TPU v7x, 32 devices: a whole 2x2x4 slice. The times are simulated.
32 devices in a mesh: seq: 8 (over z, y), slide: 4 (over x, core).
Axes of the slice: x: 2, y: 2, z: 4, core: 2. Of those that a mesh axis runs over, the one named last changes fastest.
Arguments:
- tile_embed: bfloat16 [4096, 1536], P(('seq', 'slide')), may hold values from -6 to 6
- destination: int32 [4096], P(('seq', 'slide')), may hold values from 0 to 4095, as said below
- slide_lengths: int32 [4], replicated, may hold values from 32 to 2048, as said below
- w_inner: bfloat16 [1536, 3072], replicated, may hold values from -0.15625 to 0.15625
- w_gate: bfloat16 [1536, 3072], replicated, may hold values from -0.15625 to 0.15625
- conv_weight: float32 [2, 4, 3072], replicated, may hold values from -2 to 2
- conv_bias: float32 [2, 3072], replicated, may hold values from -2 to 2
- x_project: bfloat16 [2, 3072, 128], replicated, may hold values from -0.109375 to 0.109375
- dt_project: bfloat16 [2, 96, 3072], replicated, may hold values from -0.625 to 0.625
- dt_bias: float32 [2, 3072], replicated, may hold values from -6 to -3.5
- decay: float32 [2, 16, 3072], replicated, may hold values from 0.009765625 to 32
- skip_gain: float32 [2, 3072], replicated, may hold values from 0.5 to 1.5
Outputs:
- mixed: bfloat16 [4096, 3072], P(('seq', 'slide'))
Inputs may be any that keep to these rules, and one draw needn't show every extreme that they name: `destination`: a permutation; the tile in row b of the 128 rows of each encoder device has a packed position from b * 32 to (b + 1) * 32 - 1. `slide_lengths`: each a multiple of 32; they sum to 4096; the longest is exactly 2048.
All inputs are finite; a program needn't handle non-finite values.
Results may differ from a plain program's by a relative error of at most 0.0067.
Values may be sent and summed in bfloat16 or wider, within the bound.
A program may use at most 320 MiB of HBM per device.

v0:
```python
import jax
import jax.numpy as jnp
from jax import lax
from jax.sharding import PartitionSpec as P


def with_halo(array, sides, width):
    for axis, dim in sides:
        size, length = (lax.axis_size(axis), array.shape[dim])
        up = [(i, (i + 1) % size) for i in range(size - 1)]
        down = [(j, i) for i, j in up]
        last = lax.slice_in_dim(array, length - width, length, axis=dim)
        first = lax.slice_in_dim(array, 0, width, axis=dim)
        before = lax.ppermute(last, axis, up)
        after = lax.ppermute(first, axis, down)
        array = jnp.concatenate([before, array, after], axis=dim)
    return array


def shifted(block, axis, distance):
    devices = range(lax.axis_size(axis))
    route = [(i - distance, i) for i in devices if i - distance in devices]
    return lax.ppermute(block, axis, route)


def state_sweep(start, step_size, mixed_in, b_rows, c_rows, keep, rates, reverse):
    row_count = step_size.shape[0]
    turns = 16
    per_turn = row_count // turns

    def blocked(array):
        return array.reshape((turns, per_turn) + array.shape[1:])

    def row_step(hidden, row_data):
        dt_row, u_row, b_row, c_row, keep_row = row_data
        hidden = (
            keep_row * jnp.exp(dt_row[None, :] * rates) * hidden
            + (dt_row * u_row)[None, :] * b_row[:, None]
        )
        return (hidden, jnp.sum(c_row[:, None] * hidden, axis=0))

    def block_step(hidden, block_data):
        return lax.scan(row_step, hidden, block_data, reverse=reverse, unroll=True)

    block_data = (
        blocked(step_size),
        blocked(mixed_in),
        blocked(b_rows),
        blocked(c_rows),
        blocked(keep),
    )
    last_state, outputs = lax.scan(block_step, start, block_data, reverse=reverse)
    return (last_state, outputs.reshape(row_count, -1))


def entering_rows(enter, step_size, c_rows, alive, rates, reverse):
    summed_dt = lax.cumsum(step_size, axis=0, reverse=reverse)
    added = jnp.zeros_like(step_size)
    for state in range(rates.shape[0]):
        added = (
            added
            + c_rows[:, state : state + 1]
            * jnp.exp(summed_dt * rates[state][None, :])
            * enter[state][None, :]
        )
    return added * alive[:, None]


def direction_terms(mixed_in, x_proj, dt_proj, bias, states):
    rank = dt_proj.shape[0]
    project = jnp.dot(mixed_in, x_proj, preferred_element_type=jnp.float32)
    low = project[:, :rank].astype(jnp.bfloat16)
    b_rows = project[:, rank : rank + states]
    c_rows = project[:, rank + states :]
    step_size = jax.nn.softplus(
        jnp.dot(low, dt_proj, preferred_element_type=jnp.float32) + bias[None, :]
    )
    return (step_size, b_rows, c_rows)


def slide_bounds(where_at, offsets, lengths, slide_ids):
    which = jnp.sum((where_at[:, None] >= offsets[None, 1:]).astype(jnp.int32), axis=1)
    pick = (which[:, None] == slide_ids[None, :]).astype(jnp.int32)
    begin = jnp.sum(pick * offsets[None, :], axis=1)
    return (begin, begin + jnp.sum(pick * lengths[None, :], axis=1))


def local(
    tile_embed,
    destination,
    slide_lengths,
    w_inner,
    w_gate,
    conv_weight,
    conv_bias,
    x_project,
    dt_project,
    dt_bias,
    decay,
    skip_gain,
):
    shards = lax.axis_size(("seq", "slide"))
    seq_count = lax.axis_size("seq")
    slide_count = lax.axis_size("slide")
    row_count = tile_embed.shape[0]
    model_width = tile_embed.shape[1]
    capacity = 2 * row_count
    width = w_inner.shape[1]
    states = decay.shape[1]
    taps = conv_weight.shape[1]
    slide_ids = jnp.arange(slide_lengths.shape[0], dtype=jnp.int32)
    offsets = jnp.cumsum(slide_lengths) - slide_lengths
    my_seq = lax.axis_index("seq")
    my_slide = lax.axis_index("slide")
    device_ids = jnp.arange(shards, dtype=jnp.int32)
    per_peer = capacity // shards
    slot_index = jnp.arange(per_peer, dtype=jnp.int32)
    device_slide = device_ids % slide_count
    device_seq = device_ids // slide_count
    device_pick = (device_slide[:, None] == slide_ids[None, :]).astype(jnp.int32)
    device_start = jnp.sum(device_pick * offsets[None, :], axis=1) + device_seq * capacity
    device_fill = jnp.clip(
        jnp.sum(device_pick * slide_lengths[None, :], axis=1) - device_seq * capacity, 0, capacity
    )
    first_block = device_start // shards
    live = slot_index[None, :] < (device_fill // shards)[:, None]
    safe_row = jnp.where(live, first_block[:, None] + slot_index[None, :], 0).reshape(-1)
    live_flat = live.reshape(-1)
    mine = slide_ids == my_slide
    my_start = jnp.sum(jnp.where(mine, offsets, 0)) + my_seq * capacity
    my_fill = jnp.clip(jnp.sum(jnp.where(mine, slide_lengths, 0)) - my_seq * capacity, 0, capacity)
    global_pos = my_start + jnp.arange(capacity, dtype=jnp.int32)
    row_begin = global_pos - taps
    row_end = global_pos + taps
    row_offset, _ = slide_bounds(destination, offsets, slide_lengths, slide_ids)
    row_slide = jnp.sum((destination[:, None] >= offsets[None, 1:]).astype(jnp.int32), axis=1)
    row_seq = (destination - row_offset) // capacity
    row_device = row_seq * slide_count + row_slide
    row_slot = destination // shards - (row_offset + row_seq * capacity) // shards
    send_dest = jnp.where(live_flat, jnp.take(destination, safe_row), -1).reshape(shards, per_peer)
    picked = jnp.take(tile_embed, safe_row, axis=0)
    send_rows = jnp.where(live_flat[:, None], picked, jnp.zeros_like(picked)).reshape(
        shards, per_peer, model_width
    )
    rows_in = lax.all_to_all(send_rows, ("seq", "slide"), split_axis=0, concat_axis=0, tiled=True)
    dest_in = lax.all_to_all(send_dest, ("seq", "slide"), split_axis=0, concat_axis=0, tiled=True)
    flat_rows = rows_in.reshape(-1, rows_in.shape[2])
    result = jnp.dot(flat_rows, w_inner, preferred_element_type=jnp.float32).astype(jnp.bfloat16)
    arrived = result.reshape(rows_in.shape[0], rows_in.shape[1], width)
    local_slot = dest_in - my_start
    slot_live = (dest_in >= 0) & (local_slot >= 0) & (local_slot < capacity)
    sort_key = jnp.where(slot_live, local_slot, capacity).reshape(-1)
    order = jnp.argsort(sort_key, stable=True)
    inner_rows = jnp.take(arrived.reshape(shards * per_peer, width), order, axis=0)
    padded = with_halo(inner_rows, (("seq", 0),), taps - 1)
    positions = jnp.arange(capacity, dtype=jnp.int32)
    valid = (positions < my_fill)[:, None]
    forward_sum = conv_bias[0][None, :]
    backward_sum = conv_bias[1][None, :]
    for tap in range(taps):
        ahead_ok = (global_pos - (taps - 1) + tap >= row_begin)[:, None]
        forward_sum = forward_sum + conv_weight[0, tap][None, :] * jnp.where(
            ahead_ok, padded[tap : tap + capacity], 0.0
        )
        lead = 2 * (taps - 1) - tap
        behind_ok = (global_pos + (taps - 1) - tap < row_end)[:, None]
        backward_sum = backward_sum + conv_weight[1, tap][None, :] * jnp.where(
            behind_ok, padded[lead : lead + capacity], 0.0
        )
    u_fwd = jnp.where(valid, jax.nn.silu(forward_sum), 0.0).astype(jnp.bfloat16)
    u_bwd = jnp.where(valid, jax.nn.silu(backward_sum), 0.0).astype(jnp.bfloat16)
    dt_fwd, b_fwd, c_fwd = direction_terms(u_fwd, x_project[0], dt_project[0], dt_bias[0], states)
    dt_bwd, b_bwd, c_bwd = direction_terms(u_bwd, x_project[1], dt_project[1], dt_bias[1], states)
    rates_fwd = -decay[0]
    rates_bwd = -decay[1]
    mixed_fwd = u_fwd.astype(jnp.float32)
    mixed_bwd = u_bwd.astype(jnp.float32)
    keep_fwd = (global_pos != row_begin).astype(jnp.float32)
    keep_bwd = (global_pos != row_end - 1).astype(jnp.float32)
    alive_fwd = lax.cumprod(keep_fwd, axis=0)
    alive_bwd = lax.cumprod(keep_bwd, axis=0, reverse=True)
    empty = jnp.zeros((states, width), jnp.float32)
    local_fwd, rows_fwd = state_sweep(
        empty, dt_fwd, mixed_fwd, b_fwd, c_fwd, keep_fwd, rates_fwd, False
    )
    local_bwd, rows_bwd = state_sweep(
        empty, dt_bwd, mixed_bwd, b_bwd, c_bwd, keep_bwd, rates_bwd, True
    )
    pass_fwd = jnp.exp(rates_fwd * jnp.sum(dt_fwd, axis=0)[None, :]) * alive_fwd[capacity - 1]
    pass_bwd = jnp.exp(rates_bwd * jnp.sum(dt_bwd, axis=0)[None, :]) * alive_bwd[0]

    def relay_step(turn, carried):
        from_below, from_above = carried
        from_below = shifted(pass_fwd * from_below + local_fwd, "seq", 1)
        from_above = shifted(pass_bwd * from_above + local_bwd, "seq", -1)
        return (from_below, from_above)

    enter_fwd, enter_bwd = lax.fori_loop(0, seq_count - 1, relay_step, (empty, empty))
    y_fwd = (
        rows_fwd
        + entering_rows(enter_fwd, dt_fwd, c_fwd, alive_fwd, rates_fwd, False)
        + skip_gain[0][None, :] * mixed_fwd
    )
    y_bwd = (
        rows_bwd
        + entering_rows(enter_bwd, dt_bwd, c_bwd, alive_bwd, rates_bwd, True)
        + skip_gain[1][None, :] * mixed_bwd
    )
    total = (y_fwd + y_bwd).astype(jnp.bfloat16)
    back_index = jnp.clip(local_slot, 0, capacity - 1).reshape(-1)
    send_back = jnp.take(total, back_index, axis=0).reshape(shards, per_peer, width)
    returned = lax.all_to_all(send_back, ("seq", "slide"), split_axis=0, concat_axis=0, tiled=True)
    gathered = jnp.take(
        returned.reshape(shards * per_peer, width), row_device * per_peer + row_slot, axis=0
    )
    gate = jnp.dot(tile_embed, w_gate, preferred_element_type=jnp.float32)
    return (gathered.astype(jnp.float32) * jax.nn.silu(gate)).astype(jnp.bfloat16)


def solution(mesh):
    placed = (
        P(("seq", "slide"), None),
        P(("seq", "slide")),
        P(),
        P(),
        P(),
        P(),
        P(),
        P(),
        P(),
        P(),
        P(),
        P(),
    )
    return jax.shard_map(
        local, mesh=mesh, in_specs=placed, out_specs=P(("seq", "slide"), None), check_vma=False
    )
```

profile of v0, /device:TPU:0, one launch (start us, length us, event | category | flops | bytes accessed | tf_op | source)
XLA Modules:
  0.0 1120.0 jit_solution(16088318879984338651)
XLA Ops:
  5.9 7.3 all-to-all-start.1
  25.7 5.9 all-to-all-start
  36.4 15.9 %all-to-all-done = bf16[32,8,1536]{2,1,0:T(8,128)(2,1)} async-done(((bf16[32,8,1536]{2,1,0:T(8,128)(2,1)}), bf16[32,8,1536]{2,1,0:T(8,128)(2,1)}, u32[]{:S(2)}, u32[]{:S(2)}) %all-to-all-start) | async-done | bytes 786464 | tf_op jit(solution)/shard_map/all_to_all | solution.py:145
  52.3 6.5 convolution_convert_fusion
  75.1 5.3 select_convert_fusion
  84.6 5.3 fusion.242
  92.0 394.7 %while.43 = (s32[]{:T(128)}, f32[16,3072]{1,0:T(8,128)S(1)}, f32[16,16,3072]{2,1,0:T(8,128)}, f32[16,16]{1,0:T(8,128)}, f32[16,16,3072]{2,1,0:T(8,128)}, /*index...) while((s32[]{:T(128)}, f32[16,3072]{1,0:T(8,128)S(1)}, ...), condition=%wide.region_25.27_spmd.clone, body=%wide.region_8.26_spmd.clone.sunk | while | flops 8306706 | bytes 6570068 | solution.py:52
  96.5 11.0 multiply_reduce_fusion.42
  121.3 11.0 multiply_reduce_fusion.42
  145.9 11.0 multiply_reduce_fusion.42
  170.4 11.0 multiply_reduce_fusion.42
  195.3 11.0 multiply_reduce_fusion.42
  219.9 11.0 multiply_reduce_fusion.42
  244.5 11.0 multiply_reduce_fusion.42
  269.1 11.0 multiply_reduce_fusion.42
  293.9 11.0 multiply_reduce_fusion.42
  318.6 11.0 multiply_reduce_fusion.42
  343.2 11.0 multiply_reduce_fusion.42
  367.8 11.0 multiply_reduce_fusion.42
  392.4 11.0 multiply_reduce_fusion.42
  417.1 11.0 multiply_reduce_fusion.42
  441.8 11.0 multiply_reduce_fusion.42
  466.7 11.0 multiply_reduce_fusion.42
  486.7 6.0 fusion.243
  496.9 389.8 %while.44 = (s32[]{:T(128)}, f32[16,3072]{1,0:T(8,128)S(1)}, f32[16,16,3072]{2,1,0:T(8,128)}, f32[16,16]{1,0:T(8,128)}, f32[16,16,3072]{2,1,0:T(8,128)}, /*index...) while((s32[]{:T(128)}, f32[16,3072]{1,0:T(8,128)S(1)}, ...), condition=%wide.region_51.53_spmd.clone, body=%wide.region_34.52_spmd.clone.sunk | while | flops 8306707 | bytes 6176364 | solution.py:52
  505.1 4.9 multiply_reduce_fusion.48
  529.3 4.9 multiply_reduce_fusion.48
  553.4 4.9 multiply_reduce_fusion.48
  602.2 4.9 multiply_reduce_fusion.48
  626.7 4.9 multiply_reduce_fusion.48
  651.0 4.9 multiply_reduce_fusion.48
  675.2 4.9 multiply_reduce_fusion.48
  699.7 4.9 multiply_reduce_fusion.48
  724.1 4.9 multiply_reduce_fusion.48
  748.6 4.9 multiply_reduce_fusion.48
  773.1 4.9 multiply_reduce_fusion.48
  888.1 96.4 %while.42 = (s32[]{:T(128)}, f32[16,3072]{1,0:T(8,128)S(1)}, f32[16,3072]{1,0:T(8,128)S(1)}, f32[16,3072]{1,0:T(8,128)S(1)}, f32[16,3072]{1,0:T(8,128)S(1)}, /*i...) while((s32[]{:T(128)}, f32[16,3072]{1,0:T(8,128)S(1)}, f32[16,3072]{1,0:T(8,128)S(1)}, ...), condition=%wide.region_53.55_spmd, body=%wide.region_52.54_spmd.sunk | while | flops 196610 | bytes 3145893 | solution.py:198
  908.8 6.1 collective-permute-done.1
  922.7 6.1 collective-permute-done.1
  936.6 6.1 collective-permute-done.1
  950.4 6.1 collective-permute-done.1
  964.3 6.1 collective-permute-done.1
  978.2 6.1 collective-permute-done.1
  986.1 5.2 compare_select_fusion.2
  1003.1 28.4 %fusion.202 = f32[3072,2,128]{0,1,2:T(2,128)S(1)} fusion(f32[3072,2,128]{0,2,1:T(8,128)S(1)} %bitcast.1133), kind=kOutput, calls=%fused_computation.454 | output fusion | flops 99876864 | bytes 6291456 | tf_op jit(solution)/shard_map/reduce-window.7
  1038.1 28.3 %fusion.70 = bf16[256,3072]{1,0:T(8,128)(2,1)S(1)} fusion(f32[3072,2,128]{0,2,1:T(8,128)} %copy.48, f32[16,16,3072]{2,1,0:T(8,128)} %get-tuple-element.278, f32[3072,2,128]{0,2,1:T(8,128)} %copy.44, f32[16,16,3072]{2,1,0:T(8,128)} %get-tuple-element.274, f32[3072]{0:T(1024)} %bitcast.1368, f32[256]{0:T(256)} %copy-done.60, f32[3072]{0:T(1024)S(1)} %bitcast.1336, ...), kind=kLoop, calls=%fused_computation.281 | loop fusion | flops 108527616 | bytes 18147328 | tf_op jit(solution)/shard_map/convert_element_type | solution.py:209
  1075.1 37.4 %all-to-all-done.2 = bf16[32,8,3072]{2,1,0:T(8,128)(2,1)S(1)} async-done(((bf16[32,8,3072]{2,1,0:T(8,128)(2,1)}), bf16[32,8,3072]{2,1,0:T(8,128)(2,1)S(1)}, u32[]{:S(2)}, u32[]{:S(2)}) %all-to-all-start.2) | async-done | bytes 1572896 | tf_op jit(solution)/shard_map/all_to_all | solution.py:212
  1113.6 6.3 multiply_convert_fusion
  (1118 shorter events, 687.4 us)
Async XLA Ops:
  0.0 14.0 %copy-start = (bf16[128,1536]{1,0:T(8,128)(2,1)S(1)}, bf16[128,1536]{1,0:T(8,128)(2,1)}, u32[]{:S(2)}) copy-start(bf16[128,1536]{1,0:T(8,128)(2,1)} %param.20) | copy-start | bytes 1179652
  5.9 19.8 %all-to-all-start.1 = ((s32[32,1,8]{2,1,0:T(1,128)}), s32[32,1,8]{2,1,0:T(1,128)S(1)}, u32[]{:S(2)}, u32[]{:S(2)}) async-start(s32[32,1,8]{2,1,0:T(1,128)} %bitcast.3), calls=%async_computation.1 | async-start | bytes 32768 | tf_op jit(solution)/shard_map/all_to_all | solution.py:146
  14.1 8.2 copy-start.15
  16.8 19.6 %copy-start.59 = (f32[256]{0:T(256)}, f32[256]{0:T(256)S(1)}, u32[]{:S(2)}) copy-start(f32[256]{0:T(256)S(1)} %multiply_bitcast_fusion.1) | copy-start | bytes 3076
  20.6 15.8 %copy-start.60 = (f32[256]{0:T(256)}, f32[256]{0:T(256)S(1)}, u32[]{:S(2)}) copy-start(f32[256]{0:T(256)S(1)} %multiply_bitcast_fusion) | copy-start | bytes 3076
  25.7 26.6 %all-to-all-start = ((bf16[32,8,1536]{2,1,0:T(8,128)(2,1)}), bf16[32,8,1536]{2,1,0:T(8,128)(2,1)}, u32[]{:S(2)}, u32[]{:S(2)}) async-start(bf16[32,8,1536]{2,1,0:T(8,128)(2,1)} %fusion.221), calls=%async_computation | async-start | bytes 1572864 | tf_op jit(solution)/shard_map/all_to_all | solution.py:145
  61.6 11.6 %copy-start.8 = (bf16[2,3072,128]{2,1,0:T(8,128)(2,1)S(1)}, bf16[2,3072,128]{2,1,0:T(8,128)(2,1)}, u32[]{:S(2)}) copy-start(bf16[2,3072,128]{2,1,0:T(8,128)(2,1)} %param.27) | copy-start | bytes 4718596
  63.3 5.8 collective-permute-start.2
  67.4 7.7 collective-permute-start.3
  73.1 9.2 copy-start.2
  80.4 4.0 copy-start.4
  80.4 4.1 copy-start.12
  81.1 3.6 copy-start.55
  81.1 3.6 copy-start.61
  92.0 394.7 %copy-start.54 = (f32[1,3072]{1,0:T(1,128)S(1)}, f32[1,3072]{1,0:T(1,128)}, u32[]{:S(2)}) copy-start(f32[1,3072]{1,0:T(1,128)} %get-tuple-element.859) | copy-start | bytes 36868
  486.7 6.0 copy-start.5
  496.9 389.8 %copy-start.56 = (f32[3072]{0:T(1024)S(1)}, f32[3072]{0:T(1024)}, u32[]{:S(2)}) copy-start(f32[3072]{0:T(1024)} %get-tuple-element.736) | copy-start | bytes 36868
  888.1 8.1 collective-permute-start
  892.8 8.3 collective-permute-start.1
  901.1 7.7 collective-permute-start
  905.7 9.2 collective-permute-start.1
  915.0 7.7 collective-permute-start
  919.6 9.2 collective-permute-start.1
  928.9 7.7 collective-permute-start
  933.5 9.2 collective-permute-start.1
  942.7 7.7 collective-permute-start
  947.3 9.2 collective-permute-start.1
  956.6 7.7 collective-permute-start
  961.2 9.2 collective-permute-start.1
  970.5 7.7 collective-permute-start
  975.1 9.2 collective-permute-start.1
  1034.7 3.1 copy-start.3
  1034.7 3.1 copy-start.6
  1034.7 3.1 copy-start.16
  1034.7 3.0 copy-start.17
  1034.7 3.0 copy-start.18
  1034.7 3.0 copy-start.19
  1034.8 3.0 copy-start.20
  1034.8 3.0 copy-start.21
  1034.8 3.0 copy-start.22
  1034.8 3.0 copy-start.23
  1034.8 3.0 copy-start.24
  1034.8 3.0 copy-start.25
  1034.8 3.0 copy-start.26
  1034.8 3.0 copy-start.27
  1068.1 6.7 copy-start.58
  1068.1 6.7 copy-start.1
  1070.1 42.4 %all-to-all-start.2 = ((bf16[32,8,3072]{2,1,0:T(8,128)(2,1)}), bf16[32,8,3072]{2,1,0:T(8,128)(2,1)S(1)}, u32[]{:S(2)}, u32[]{:S(2)}) async-start(bf16[32,8,3072]{2,1,0:T(8,128)(2,1)} %select_bitcast_fusion), calls=%async_computation.2 | async-start | bytes 3145728 | tf_op jit(solution)/shard_map/all_to_all | solution.py:212
  (33 other events, 90.7 us)
where the time goes:
time: 1140 us; the launch traced here: 1120 us
  other arithmetic  710 us (62%)
  local copies, waits for them, and re-layouts  205 us (18%)
  waiting for transfers between devices  108 us (9%)
  starting transfers between devices  64 us (6%)
  matrix products  25.4 us (2%)
    reduce_sum x160, other arithmetic, row_step(): return (hidden, jnp.sum(c_row[:, None] * hidden, axis=0))  603 us
    slice x64, local copies, waits for them, and re-layouts, block_step(): return lax.scan(row_step, hidden, block_data, reverse=reverse, unroll=True)  114 us
    ppermute x14, waiting for transfers between devices, shifted(): return lax.ppermute(block, axis, route)  54.6 us
    ppermute x14, starting transfers between devices, shifted(): return lax.ppermute(block, axis, route)  40.9 us
    another operation x9, other arithmetic  40.4 us
    all_to_all x1, waiting for transfers between devices, local(): lax.all_to_all(send_back, ('seq', 'slide'), split_axis=0, concat_axis=0,...  37.4 us
    convert_element_type x1, other arithmetic, local(): total = (y_fwd + y_bwd).astype(jnp.bfloat16)  28.3 us
  transfers between devices with their start and end apart: 19, of which 16 were waited for; matrix products, arithmetic and copies ran while one was open for 2% of the time, Pallas kernels for 0%

commit v1 on v0

v1 whole, which is shorter than its diff:
```python
import functools

import jax
import jax.numpy as jnp
from jax import lax
from jax.experimental import pallas as pl
from jax.experimental.pallas import tpu as pltpu
from jax.sharding import PartitionSpec as P

AXES = ("seq", "slide")
LANES = 128
SUB = 8
LOG2E = 1.4426950408889634


def slide_starts(len_ref):
    starts = [jnp.int32(0)]
    for s in range(len_ref.shape[0]):
        starts.append(starts[-1] + len_ref[s])
    return starts


def keep_at(starts, pos):
    hit = pos == starts[0]
    for s in starts[1:]:
        hit = jnp.logical_or(hit, pos == s)
    return jnp.where(hit, 0.0, 1.0).astype(jnp.float32)


def spread_rates(decay_ref, rate_scr, folds):
    count = decay_ref.shape[0]
    for k in range(folds):
        rate_scr[pl.ds(k, count, stride=folds), :] = (
            decay_ref[:, k * LANES : (k + 1) * LANES] * -LOG2E
        )


def sweep_kernel(
    states, rank, chunk,
    me_ref, len_ref, inner_ref, prev_ref, next_ref, cw_ref, cb_ref, xp_ref, dp_ref, db_ref,
    decay_ref, skip_ref,
    dt_ref, proj_ref, y_ref, pay_ref,
    pad, u_ref, rate_scr, ubf, bc, sem,
):
    rows, width = inner_ref.shape
    folds = width // LANES
    taps = cw_ref.shape[0] // 2
    halo = prev_ref.shape[0]
    starts = slide_starts(len_ref)
    base = me_ref[0] * rows
    spread_rates(decay_ref, rate_scr, folds)
    pad[0:SUB, :] = prev_ref[...].astype(jnp.float32)
    pad[SUB : SUB + rows, :] = inner_ref[...].astype(jnp.float32)
    pad[SUB + rows : 2 * SUB + rows, :] = next_ref[...].astype(jnp.float32)
    where_at = base + lax.broadcasted_iota(jnp.int32, (rows, LANES), 0)
    masks = {}
    for dist in range(1, taps):
        for sign in (-1, 1):
            bad = jnp.zeros((rows, LANES), jnp.bool_)
            for s in starts:
                if sign < 0:
                    bad = bad | ((where_at - dist < s) & (where_at >= s))
                else:
                    bad = bad | ((where_at < s) & (where_at + dist >= s))
            masks[sign * dist] = jnp.where(bad, 0.0, 1.0)
    block = LANES
    wide = 2 * LANES
    for d in range(2):
        acc = jnp.zeros((rows, LANES), jnp.float32)
        for cb in range(width // wide):
            for half in range(2):
                k = 2 * cb + half
                cols = slice(k * block, (k + 1) * block)
                total = jnp.broadcast_to(cb_ref[d : d + 1, cols], (rows, block))
                for tap in range(taps):
                    dist = (tap - (taps - 1)) if d == 0 else (taps - 1 - tap)
                    term = pad[SUB + dist : SUB + dist + rows, cols]
                    if dist != 0:
                        term = term * masks[dist]
                    total = total + cw_ref[d * taps + tap : d * taps + tap + 1, cols] * term
                u = (total / (1.0 + jnp.exp(-total))).astype(jnp.bfloat16)
                ubf[:, cols] = u
                u_ref[d, pl.ds(k, rows, stride=folds), :] = u.astype(jnp.float32)
            wcols = slice(cb * wide, (cb + 1) * wide)
            acc = acc + jnp.dot(
                ubf[:, wcols], xp_ref[d, wcols, :], preferred_element_type=jnp.float32
            )
        proj_ref[d * rows : (d + 1) * rows, :] = acc
        low = acc[:, :rank].astype(jnp.bfloat16)
        for cb in range(width // wide):
            wcols = slice(cb * wide, (cb + 1) * wide)
            v = jnp.dot(low, dp_ref[d, :, wcols], preferred_element_type=jnp.float32)
            v = v + db_ref[d : d + 1, wcols]
            step = jnp.maximum(v, 0.0) + jnp.log1p(jnp.exp(-jnp.abs(v)))
            for half in range(2):
                dt_ref[d, pl.ds(2 * cb + half, rows, stride=folds), :] = step[
                    :, half * LANES : (half + 1) * LANES
                ]
    copy = pltpu.make_async_copy(proj_ref, bc, sem)
    copy.start()
    copy.wait()
    chunks = rows // chunk
    zero = jnp.zeros((SUB, LANES), jnp.float32)
    for d in range(2):
        for j in range(folds // SUB):
            rates = [
                rate_scr[(d * states + n) * folds + j * SUB : (d * states + n) * folds + (j + 1) * SUB, :]
                for n in range(states)
            ]
            skip = skip_ref[d, j * SUB : (j + 1) * SUB, :]

            def chunk_step(ci, carry):
                hs, sdt = carry
                c = ci if d == 0 else chunks - 1 - ci
                keep = keep_at(starts, base + (c if d == 0 else c + 1) * chunk)
                hs = tuple(h * keep for h in hs)

                def row_step(i, inner_carry):
                    hs, sdt = inner_carry
                    t = c * chunk + (i if d == 0 else chunk - 1 - i)
                    spot = pl.ds(pl.multiple_of(t * folds + j * SUB, SUB), SUB)
                    dt = dt_ref[d, spot, :]
                    u = u_ref[d, spot, :]
                    dtu = dt * u
                    parts = [skip * u, None, None, None]
                    out = []
                    for n in range(states):
                        h = jnp.exp2(dt * rates[n]) * hs[n] + dtu * bc[d * rows + t, rank + n]
                        out.append(h)
                        term = h * bc[d * rows + t, rank + states + n]
                        q = n % 4
                        parts[q] = term if parts[q] is None else parts[q] + term
                    y = (parts[0] + parts[1]) + (parts[2] + parts[3])
                    if d == 0:
                        y_ref[spot, :] = y
                    else:
                        y_ref[spot, :] += y
                    return (tuple(out), sdt + dt)

                return lax.fori_loop(0, chunk, row_step, (hs, sdt), unroll=2)

            hs, sdt = lax.fori_loop(0, chunks, chunk_step, ((zero,) * states, zero))
            for n in range(states):
                pay_ref[d * states + n, j * SUB : (j + 1) * SUB, :] = hs[n]
                pay_ref[d * states + n, folds + j * SUB : folds + (j + 1) * SUB, :] = sdt


def relay_kernel(states, split, rows, chunk, me_ref, len_ref, got_ref, rate_ref, out_ref):
    shards = got_ref.shape[0]
    depth = got_ref.shape[1] // 2
    starts = slide_starts(len_ref)
    backward = me_ref[0] // split >= states
    rate = rate_ref[...] * -LOG2E

    def step(i, h):
        s = jnp.where(backward, shards - 1 - i, i)
        keep = jnp.float32(1.0)
        for c in range(rows // chunk):
            keep = keep * keep_at(
                starts, s * rows + c * chunk + jnp.where(backward, chunk, 0)
            )
        out_ref[s] = h.astype(jnp.bfloat16)
        got = got_ref[s].astype(jnp.float32)
        return jnp.exp2(rate * got[depth:]) * (h * keep) + got[:depth]

    lax.fori_loop(0, shards, step, jnp.zeros((depth, LANES), jnp.float32))


def finish_kernel(
    states, rank, chunk,
    me_ref, len_ref, bc, dt_ref, y_ref, enter_ref, decay_ref, slot_ref,
    out_ref,
    rate_scr, tot,
):
    rows, width = out_ref.shape
    folds = width // LANES
    chunks = rows // chunk
    starts = slide_starts(len_ref)
    base = me_ref[0] * rows
    spread_rates(decay_ref, rate_scr, folds)
    for d in range(2):
        for j in range(folds // SUB):
            rates = [
                rate_scr[(d * states + n) * folds + j * SUB : (d * states + n) * folds + (j + 1) * SUB, :]
                for n in range(states)
            ]
            enters = [
                enter_ref[d * states + n, j * SUB : (j + 1) * SUB, :].astype(jnp.float32)
                for n in range(states)
            ]

            def chunk_step(ci, carry):
                alive, sdt = carry
                c = ci if d == 0 else chunks - 1 - ci
                alive = alive * keep_at(starts, base + (c if d == 0 else c + 1) * chunk)

                def row_step(i, sdt):
                    t = c * chunk + (i if d == 0 else chunk - 1 - i)
                    spot = pl.ds(pl.multiple_of(t * folds + j * SUB, SUB), SUB)
                    sdt = sdt + dt_ref[d, spot, :]
                    parts = [None] * 4
                    for n in range(states):
                        term = jnp.exp2(sdt * rates[n]) * (
                            enters[n] * bc[d * rows + t, rank + states + n]
                        )
                        q = n % 4
                        parts[q] = term if parts[q] is None else parts[q] + term
                    y = ((parts[0] + parts[1]) + (parts[2] + parts[3])) * alive
                    if d == 0:
                        tot[spot, :] = y_ref[spot, :] + y
                    else:
                        tot[spot, :] += y
                    return sdt

                return (alive, lax.fori_loop(0, chunk, row_step, sdt, unroll=2))

            lax.fori_loop(
                0, chunks, chunk_step, (jnp.float32(1.0), jnp.zeros((SUB, LANES), jnp.float32))
            )
    pick = (
        slot_ref[...] == lax.broadcasted_iota(jnp.int32, (rows, rows), 1)
    ).astype(jnp.bfloat16)
    for k in range(folds):
        part = tot[pl.ds(k, rows, stride=folds), :].astype(jnp.bfloat16)
        out_ref[:, k * LANES : (k + 1) * LANES] = jnp.dot(
            pick, part, preferred_element_type=jnp.float32
        ).astype(jnp.bfloat16)


def local(
    tile_embed, destination, slide_lengths, w_inner, w_gate, conv_weight, conv_bias, x_project,
    dt_project, dt_bias, decay, skip_gain,
):
    shards = lax.axis_size(AXES)
    rows, model = tile_embed.shape
    width = w_inner.shape[1]
    states = decay.shape[1]
    rank = dt_project.shape[1]
    taps = conv_weight.shape[1]
    folds = width // LANES
    per_peer = rows // shards
    chunk = min(shards, rows)
    split = shards // (2 * states)
    halo = taps - 1
    me = lax.axis_index(AXES).astype(jnp.int32)
    me_arr = me[None]
    f32, bf16 = jnp.float32, jnp.bfloat16
    vmem = pl.BlockSpec(memory_space=pltpu.VMEM)
    smem = pl.BlockSpec(memory_space=pltpu.SMEM)
    params = pltpu.CompilerParams(vmem_limit_bytes=48 * 1024 * 1024)

    slot_col = jnp.broadcast_to((destination % rows).astype(bf16)[:, None], (rows, LANES))
    sent = jnp.concatenate([tile_embed, slot_col], axis=1).reshape(shards, per_peer, model + LANES)
    got = lax.all_to_all(sent, AXES, split_axis=0, concat_axis=0, tiled=True)
    got = got.reshape(rows, model + LANES)
    slot = got[:, model].astype(jnp.int32)
    place = (slot[None, :] == jnp.arange(rows, dtype=jnp.int32)[:, None]).astype(bf16)
    ordered = jnp.dot(place, got[:, :model], preferred_element_type=f32).astype(bf16)
    inner = jnp.dot(ordered, w_inner, preferred_element_type=f32).astype(bf16)
    up = [(i, i + 1) for i in range(shards - 1)]
    down = [(i + 1, i) for i in range(shards - 1)]
    before = lax.ppermute(inner[rows - SUB :], AXES, up)
    after = lax.ppermute(inner[:SUB], AXES, down)
    dt, proj, y, pay = pl.pallas_call(
        functools.partial(sweep_kernel, states, rank, chunk),
        out_shape=(
            jax.ShapeDtypeStruct((2, rows * folds, LANES), f32),
            jax.ShapeDtypeStruct((2 * rows, LANES), f32),
            jax.ShapeDtypeStruct((rows * folds, LANES), f32),
            jax.ShapeDtypeStruct((2 * states, 2 * folds, LANES), f32),
        ),
        in_specs=[smem, smem] + [vmem] * 10,
        out_specs=(vmem,) * 4,
        scratch_shapes=[
            pltpu.VMEM((rows + 2 * SUB, width), f32),
            pltpu.VMEM((2, rows * folds, LANES), f32),
            pltpu.VMEM((2 * states * folds, LANES), f32),
            pltpu.VMEM((rows, width), bf16),
            pltpu.SMEM((2 * rows, LANES), f32),
            pltpu.SemaphoreType.DMA,
        ],
        compiler_params=params,
        name="sweep",
    )(
        me_arr, slide_lengths, inner, before, after, conv_weight.reshape(2 * taps, width), conv_bias,
        x_project, dt_project, dt_bias, decay.reshape(2 * states, width),
        skip_gain.reshape(2, folds, LANES),
    )
    pay = pay.astype(bf16).reshape(2 * states, 2, split, folds // split, LANES)
    pay = pay.swapaxes(1, 2).reshape(shards, 2 * folds // split, LANES)
    theirs = lax.all_to_all(pay, AXES, split_axis=0, concat_axis=0, tiled=True)
    my_rate = lax.dynamic_slice_in_dim(
        decay.reshape(shards, folds // split, LANES), me, 1, axis=0
    )[0]
    enter = pl.pallas_call(
        functools.partial(relay_kernel, states, split, rows, chunk),
        out_shape=jax.ShapeDtypeStruct((shards, folds // split, LANES), bf16),
        in_specs=[smem, smem, vmem, vmem],
        out_specs=vmem,
        compiler_params=params,
        name="relay",
    )(me_arr, slide_lengths, theirs, my_rate)
    enter = lax.all_to_all(enter, AXES, split_axis=0, concat_axis=0, tiled=True)
    enter = enter.reshape(2 * states, folds, LANES)
    back = pl.pallas_call(
        functools.partial(finish_kernel, states, rank, chunk),
        out_shape=jax.ShapeDtypeStruct((rows, width), bf16),
        in_specs=[smem, smem, smem] + [vmem] * 5,
        out_specs=vmem,
        scratch_shapes=[
            pltpu.VMEM((2 * states * folds, LANES), f32),
            pltpu.VMEM((rows * folds, LANES), f32),
        ],
        compiler_params=params,
        name="finish",
    )(
        me_arr, slide_lengths, proj, dt, y, enter, decay.reshape(2 * states, width),
        slot[:, None],
    )
    back = back.reshape(shards, per_peer, width)
    returned = lax.all_to_all(back, AXES, split_axis=0, concat_axis=0, tiled=True)
    gate = jnp.dot(tile_embed, w_gate, preferred_element_type=f32)
    return (returned.reshape(rows, width).astype(f32) * jax.nn.silu(gate)).astype(bf16)


def solution(mesh):
    placed = (P(AXES, None), P(AXES)) + (P(),) * 10
    return jax.shard_map(
        local, mesh=mesh, in_specs=placed, out_specs=P(AXES, None), check_vma=False
    )
```

time: 1140 us -> 150 us (0.13); the launches traced: 1120 us -> 150 us
  other arithmetic: 710 us -> 3.37 us
  local copies, waits for them, and re-layouts: 205 us -> 3 us
  waiting for transfers between devices: 108 us -> 22 us
  Pallas kernels: 0 us -> 52.1 us
  starting transfers between devices: 64 us -> 13.5 us
  blocking collectives: 0 us -> 44 us
  matrix products: 25.4 us -> 11.5 us
    reduce_sum x164 -> x0, other arithmetic: 605 us -> none  [the longest x160 603 us: row_step(): return (hidden, jnp.sum(c_row[:, None] * hidden, axis=0))]
    slice x80 -> x1, local copies, waits for them, and re-layouts: 123 us -> 0.01 us  [local(): after = lax.ppermute(inner[:SUB], AXES, down)]
    ppermute x16 -> x2, waiting for transfers between devices: 54.6 us -> 0.76 us  [the longest x1 0.76 us: local(): before = lax.ppermute(inner[rows - SUB:], AXES, up)]
    pallas_call x0 -> x3, Pallas kernels: none -> 52.1 us  [the longest x1 32.1 us: local(): pl.pallas_call(functools.partial(sweep_kernel, states, rank, chunk), out_...]
    all_to_all x0 -> x2, blocking collectives: none -> 44 us  [the longest x1 23.1 us: local(): lax.all_to_all(back, AXES, split_axis=0, concat_axis=0, tiled=True)]
    ppermute x16 -> x2, starting transfers between devices: 46.1 us -> 4.32 us  [the longest x1 3.03 us: local(): before = lax.ppermute(inner[rows - SUB:], AXES, up)]
    another operation x11 -> x0, other arithmetic: 41.1 us -> none
    convert_element_type x5 -> x4, other arithmetic: 38.2 us -> 2.34 us  [the longest x2 0.87 us: local(): slot = got[:, model].astype(jnp.int32)]
  transfers between devices with their start and end apart: 19 -> 4, of which waited for: 16 -> 3; matrix products, arithmetic and copies ran while one was open for 2% -> 1% of each run, Pallas kernels for 0% -> 0%
where the time goes in v1:
time: 150 us
  Pallas kernels  52.1 us (35%)
  blocking collectives  44 us (29%)
  waiting for transfers between devices  22 us (15%)
  starting transfers between devices  13.5 us (9%)
  matrix products  11.5 us (8%)
  other arithmetic  3.37 us (2%)
  local copies, waits for them, and re-layouts  3 us (2%)
    pallas_call x1, Pallas kernels, local(): pl.pallas_call(functools.partial(sweep_kernel, states, rank, chunk), out_...  32.1 us
    all_to_all x1, blocking collectives, local(): lax.all_to_all(back, AXES, split_axis=0, concat_axis=0, tiled=True)  23.1 us
    all_to_all x1, blocking collectives, local(): got = lax.all_to_all(sent, AXES, split_axis=0, concat_axis=0, tiled=True)  20.9 us
    pallas_call x1, Pallas kernels, local(): pl.pallas_call(functools.partial(finish_kernel, states, rank, chunk), out...  18 us
    all_to_all x1, waiting for transfers between devices, local(): theirs = lax.all_to_all(pay, AXES, split_axis=0, concat_axis=0, tiled=True)  13.1 us
    all_to_all x1, waiting for transfers between devices, local(): enter = lax.all_to_all(enter, AXES, split_axis=0, concat_axis=0, tiled=True)  8.12 us
    all_to_all x1, starting transfers between devices, local(): theirs = lax.all_to_all(pay, AXES, split_axis=0, concat_axis=0, tiled=True)  6.53 us
    dot_general x1, matrix products, local(): gate = jnp.dot(tile_embed, w_gate, preferred_element_type=f32)  6.19 us
  transfers between devices with their start and end apart: 4, of which 3 were waited for; matrix products, arithmetic and copies ran while one was open for 1% of the time, Pallas kernels for 0%

profile of v1, /device:TPU:0, one launch (start us, length us, event | category | flops | bytes accessed | tf_op | source)
XLA Modules:
  0.0 149.6 jit_solution(14851745159851617187)
XLA Ops:
  0.0 0.7 fusion.5
  0.7 0.1 broadcast_in_dim.5
  0.8 1.0 pad_maximum_fusion
  1.8 0.1 reshape.33
  1.9 20.9 %all_to_all.20 = bf16[32,4,1664]{2,1,0:T(4,128)(2,1)S(1)} all-to-all(bf16[32,4,1664]{2,1,0:T(4,128)(2,1)S(1)} %reshape.33), channel_id=1, replica_groups=mesh['seq'=8,'slide'=4] {'seq','slide'}, dimensions={0} | all-to-all | bytes 851968 | tf_op jit(solution)/shard_map/all_to_all | solution.py:254
  22.8 0.1 reshape.34
  22.9 0.0 copy-start.5
  22.9 0.1 fusion.4
  23.0 0.0 copy-start.8
  23.0 0.0 copy-start.7
  23.0 0.0 copy-start
  23.0 0.0 copy-start.2
  23.0 0.0 copy-start.3
  23.1 0.0 copy-start.4
  23.1 5.3 %convolution_convert_fusion.inner_ref = bf16[128,3072]{1,0:T(8,128)(2,1)S(1)} fusion(bf16[1536,3072]{1,0:T(8,128)(2,1)} %param.15, bf16[128,1664]{1,0:T(8,128)(2,1)S(1)} %reshape.34, s32[128]{0:T(128)S(1)} %fusion.4), kind=kOutput, calls=%fused_computation | convolution fusion | flops 1258897408 | bytes 10617344 | tf_op jit(solution)/shard_map/dot_general | solution.py:259
  28.3 0.0 copy-done.5
  28.4 1.3 collective-permute-start.1
  29.7 3.0 %collective-permute-start = (bf16[8,3072]{1,0:T(8,128)(2,1)S(1)}, bf16[8,3072]{1,0:T(8,128)(2,1)S(1)}, u32[]{:S(2)}, u32[]{:S(2)}) collective-permute-start(bf16[8,3072]{1,0:T(8,128)(2,1)S(1)} %get-tuple-element.14), channel_id=1, source_target_pairs={{0,1},{1,2},{2,3},{3,4},{4,5},{5,6},{6,7},{7,8},{8,9},{9,10},{10,1... | collective-permute-start | bytes 147464 | tf_op jit(solution)/shard_map/ppermute | solution.py:262
  32.7 0.0 copy-done.8
  32.7 0.0 copy-done.7
  32.8 0.0 collective-permute-done.1.next_ref
  32.8 0.8 collective-permute-done.prev_ref
  33.6 0.0 copy-done
  33.6 0.0 copy-done.2
  33.6 0.0 copy-done.3
  33.6 0.0 copy-done.4
  33.6 0.0 copy-start.1
  33.6 1.3 copy-done.1
  34.9 32.1 %sweep.1 = (f32[2,3072,128]{2,1,0:T(8,128)}, f32[256,128]{1,0:T(8,128)S(1)}, f32[3072,128]{1,0:T(8,128)S(1)}, f32[32,48,128]{2,1,0:T(8,128)S(1)}) custom-call(s32[1]{0:T(128)} %bitcast.me_ref, s32[4]{0:T(128)S(1)} %copy-done.4, bf16[128,3072]{1,0:T(8,128)(2,1)S(1)} %convolution_convert_fusion.inner_ref, bf16[8,3072]{1,0:T(8,128)(2,1)S(1)} %collective-permute-done.prev_ref, ...), custom_call_target="tpu_custom_call" | custom-call | tf_op jit(solution)/shard_map/sweep/pallas_call | solution.py:264
  66.9 0.8 convert_element_type.40
  67.7 6.5 %all-to-all-start.1 = ((bf16[32,48,128]{2,1,0:T(8,128)(2,1)}), bf16[32,48,128]{2,1,0:T(8,128)(2,1)S(1)}, u32[]{:S(2)}, u32[]{:S(2)}) async-start(bf16[32,48,128]{2,1,0:T(8,128)(2,1)} %convert_element_type.40), calls=%async_computation.1 | async-start | bytes 786432 | tf_op jit(solution)/shard_map/all_to_all | solution.py:291
  74.3 0.1 copy.14
  74.4 13.1 %all-to-all-done.1.got_ref = bf16[32,48,128]{2,1,0:T(8,128)(2,1)S(1)} async-done(((bf16[32,48,128]{2,1,0:T(8,128)(2,1)}), bf16[32,48,128]{2,1,0:T(8,128)(2,1)S(1)}, u32[]{:S(2)}, u32[]{:S(2)}) %all-to-all-start.1) | async-done | bytes 393248 | tf_op jit(solution)/shard_map/all_to_all | solution.py:291
  87.5 2.0 %relay.1 = bf16[32,24,128]{2,1,0:T(8,128)(2,1)} custom-call(s32[1]{0:T(128)} %bitcast.me_ref, s32[4]{0:T(128)S(1)} %copy-done.4, bf16[32,48,128]{2,1,0:T(8,128)(2,1)S(1)} %all-to-all-done.1.got_ref, f32[24,128]{1,0:T(8,128)S(1)} %dynamic-slice_bitcast_fusion.rate_ref), custom_call_target="tpu_custom_call" | custom-call | tf_op jit(solution)/shard_map/relay/pallas_call | solution.py:295
  89.5 2.6 %all-to-all-start.2 = ((bf16[32,24,128]{2,1,0:T(8,128)(2,1)}), bf16[32,24,128]{2,1,0:T(8,128)(2,1)S(1)}, u32[]{:S(2)}, u32[]{:S(2)}) async-start(bf16[32,24,128]{2,1,0:T(8,128)(2,1)} %relay.1), calls=%async_computation.2 | async-start | bytes 393216 | tf_op jit(solution)/shard_map/all_to_all | solution.py:303
  92.1 0.8 slice_convert_fusion.slot_ref
  92.9 8.1 %all-to-all-done.2.enter_ref = bf16[32,24,128]{2,1,0:T(8,128)(2,1)S(1)} async-done(((bf16[32,24,128]{2,1,0:T(8,128)(2,1)}), bf16[32,24,128]{2,1,0:T(8,128)(2,1)S(1)}, u32[]{:S(2)}, u32[]{:S(2)}) %all-to-all-start.2) | async-done | bytes 196640 | tf_op jit(solution)/shard_map/all_to_all | solution.py:303
  101.0 18.0 %finish.1 = bf16[128,3072]{1,0:T(8,128)(2,1)S(1)} custom-call(s32[1]{0:T(128)} %bitcast.me_ref, s32[4]{0:T(128)S(1)} %copy-done.4, f32[256,128]{1,0:T(8,128)S(1)} %get-tuple-element.9.bc, f32[2,3072,128]{2,1,0:T(8,128)} %get-tuple-element.10.dt_ref, f32[3072,128]{1,0:T(8,128)S(1)} %get-tuple-element.11.y_ref, ...), custom_call_target="tpu_custom_call" | custom-call | tf_op jit(solution)/shard_map/finish/pallas_call | solution.py:305
  119.0 0.3 reshape.39
  119.3 23.1 %all_to_all.21 = bf16[32,4,3072]{2,1,0:T(4,128)(2,1)S(1)} all-to-all(bf16[32,4,3072]{2,1,0:T(4,128)(2,1)S(1)} %reshape.39), channel_id=1, replica_groups=mesh['seq'=8,'slide'=4] {'seq','slide'}, dimensions={0} | all-to-all | bytes 1572864 | tf_op jit(solution)/shard_map/all_to_all | solution.py:321
  142.5 0.0 copy-start.6
  142.5 0.1 reshape.41
  142.6 0.9 copy-done.6
  143.5 6.2 %multiply_convert_fusion = bf16[128,3072]{1,0:T(8,128)(2,1)} fusion(f32[128,3072]{1,0:T(8,128)S(1)} %reshape.41, bf16[128,1536]{1,0:T(8,128)(2,1)S(1)} %copy-done.6, bf16[1536,3072]{1,0:T(8,128)(2,1)} %param.16), kind=kOutput, calls=%fused_computation.2 | convolution fusion | flops 1210318848 | bytes 12189696 | tf_op jit(solution)/shard_map/dot_general | solution.py:322
  (4 shorter events, 0.1 us)
Async XLA Ops:
  22.9 5.5 %copy-start.5 = (bf16[128,1664]{1,0:T(8,128)(2,1)}, bf16[128,1664]{1,0:T(8,128)(2,1)S(1)}, u32[]{:S(2)}) copy-start(bf16[128,1664]{1,0:T(8,128)(2,1)S(1)} %reshape.34) | copy-start | bytes 1277956
  23.0 9.7 %copy-start.8 = (f32[2,3072]{1,0:T(2,128)S(1)}, f32[2,3072]{1,0:T(2,128)}, u32[]{:S(2)}) copy-start(f32[2,3072]{1,0:T(2,128)} %param.23) | copy-start | bytes 73732
  23.0 9.7 %copy-start.7 = (f32[2,4,3072]{2,1,0:T(4,128)S(1)}, f32[2,4,3072]{2,1,0:T(4,128)}, u32[]{:S(2)}) copy-start(f32[2,4,3072]{2,1,0:T(4,128)} %param.17) | copy-start | bytes 294916
  23.0 10.6 %copy-start = (f32[2,16,3072]{2,1,0:T(8,128)S(1)}, f32[2,16,3072]{2,1,0:T(8,128)}, u32[]{:S(2)}) copy-start(f32[2,16,3072]{2,1,0:T(8,128)} %param.22) | copy-start | bytes 1179652
  23.0 10.5 %copy-start.2 = (f32[2,3072]{1,0:T(2,128)S(1)}, f32[2,3072]{1,0:T(2,128)}, u32[]{:S(2)}) copy-start(f32[2,3072]{1,0:T(2,128)} %cb_ref.1) | copy-start | bytes 73732
  23.0 10.5 %copy-start.3 = (f32[2,3072]{1,0:T(2,128)S(1)}, f32[2,3072]{1,0:T(2,128)}, u32[]{:S(2)}) copy-start(f32[2,3072]{1,0:T(2,128)} %db_ref.1) | copy-start | bytes 73732
  23.1 10.5 %copy-start.4 = (s32[4]{0:T(128)S(1)}, s32[4]{0:T(128)}, u32[]{:S(2)}) copy-start(s32[4]{0:T(128)} %len_ref.5) | copy-start | bytes 52
  28.4 4.4 %collective-permute-start.1 = (bf16[8,3072]{1,0:T(8,128)(2,1)S(1)}, bf16[8,3072]{1,0:T(8,128)(2,1)S(1)}, u32[]{:S(2)}, u32[]{:S(2)}) collective-permute-start(bf16[8,3072]{1,0:T(8,128)(2,1)S(1)} %get-tuple-element.13), channel_id=1, source_target_pairs={{1,0},{2,1},{3,2},{4,3},{5,4},{6,5},{7,6},{8,7},{9,8},{10,9},{11,1... | collective-permute-start | bytes 147464 | tf_op jit(solution)/shard_map/ppermute | solution.py:263
  29.7 3.9 %collective-permute-start = (bf16[8,3072]{1,0:T(8,128)(2,1)S(1)}, bf16[8,3072]{1,0:T(8,128)(2,1)S(1)}, u32[]{:S(2)}, u32[]{:S(2)}) collective-permute-start(bf16[8,3072]{1,0:T(8,128)(2,1)S(1)} %get-tuple-element.14), channel_id=1, source_target_pairs={{0,1},{1,2},{2,3},{3,4},{4,5},{5,6},{6,7},{7,8},{8,9},{9,10},{10,1... | collective-permute-start | bytes 147464 | tf_op jit(solution)/shard_map/ppermute | solution.py:262
  33.6 1.3 copy-start.1
  67.7 19.7 %all-to-all-start.1 = ((bf16[32,48,128]{2,1,0:T(8,128)(2,1)}), bf16[32,48,128]{2,1,0:T(8,128)(2,1)S(1)}, u32[]{:S(2)}, u32[]{:S(2)}) async-start(bf16[32,48,128]{2,1,0:T(8,128)(2,1)} %convert_element_type.40), calls=%async_computation.1 | async-start | bytes 786432 | tf_op jit(solution)/shard_map/all_to_all | solution.py:291
  89.5 11.5 %all-to-all-start.2 = ((bf16[32,24,128]{2,1,0:T(8,128)(2,1)}), bf16[32,24,128]{2,1,0:T(8,128)(2,1)S(1)}, u32[]{:S(2)}, u32[]{:S(2)}) async-start(bf16[32,24,128]{2,1,0:T(8,128)(2,1)} %relay.1), calls=%async_computation.2 | async-start | bytes 393216 | tf_op jit(solution)/shard_map/all_to_all | solution.py:303
  142.5 1.0 copy-start.6

commit v2 on v1

--- a/solution.py
+++ b/solution.py
@@ -40,7 +40,7 @@
     me_ref, len_ref, inner_ref, prev_ref, next_ref, cw_ref, cb_ref, xp_ref, dp_ref, db_ref,
     decay_ref, skip_ref,
     dt_ref, proj_ref, y_ref, pay_ref,
-    pad, u_ref, rate_scr, ubf, bc, sem,
+    pad, u_ref, rate_scr, ubf, held, bc, sem,
 ):
     rows, width = inner_ref.shape
     folds = width // LANES
@@ -49,9 +49,9 @@
     starts = slide_starts(len_ref)
     base = me_ref[0] * rows
     spread_rates(decay_ref, rate_scr, folds)
-    pad[0:SUB, :] = prev_ref[...].astype(jnp.float32)
+    pad[0:SUB, :] = prev_ref[halo - SUB :, :].astype(jnp.float32)
     pad[SUB : SUB + rows, :] = inner_ref[...].astype(jnp.float32)
-    pad[SUB + rows : 2 * SUB + rows, :] = next_ref[...].astype(jnp.float32)
+    pad[SUB + rows : 2 * SUB + rows, :] = next_ref[0:SUB, :].astype(jnp.float32)
     where_at = base + lax.broadcasted_iota(jnp.int32, (rows, LANES), 0)
     masks = {}
     for dist in range(1, taps):
@@ -141,8 +141,9 @@
 
             hs, sdt = lax.fori_loop(0, chunks, chunk_step, ((zero,) * states, zero))
             for n in range(states):
-                pay_ref[d * states + n, j * SUB : (j + 1) * SUB, :] = hs[n]
-                pay_ref[d * states + n, folds + j * SUB : folds + (j + 1) * SUB, :] = sdt
+                held[d * states + n, j * SUB : (j + 1) * SUB, :] = hs[n]
+                held[d * states + n, folds + j * SUB : folds + (j + 1) * SUB, :] = sdt
+    pay_ref[...] = held[...].astype(jnp.bfloat16)
 
 
 def relay_kernel(states, split, rows, chunk, me_ref, len_ref, got_ref, rate_ref, out_ref):
@@ -168,12 +169,12 @@
 
 def finish_kernel(
     states, rank, chunk,
-    me_ref, len_ref, bc, dt_ref, y_ref, enter_ref, decay_ref, slot_ref,
+    me_ref, len_ref, bc, dt_ref, y_ref, enter_ref, decay_ref, place_ref,
     out_ref,
     rate_scr, tot,
 ):
-    rows, width = out_ref.shape
-    folds = width // LANES
+    rows = place_ref.shape[0]
+    folds = decay_ref.shape[1] // LANES
     chunks = rows // chunk
     starts = slide_starts(len_ref)
     base = me_ref[0] * rows
@@ -217,13 +218,192 @@
             lax.fori_loop(
                 0, chunks, chunk_step, (jnp.float32(1.0), jnp.zeros((SUB, LANES), jnp.float32))
             )
-    pick = (
-        slot_ref[...] == lax.broadcasted_iota(jnp.int32, (rows, rows), 1)
-    ).astype(jnp.bfloat16)
+    pick = place_ref[...]
     for k in range(folds):
         part = tot[pl.ds(k, rows, stride=folds), :].astype(jnp.bfloat16)
-        out_ref[:, k * LANES : (k + 1) * LANES] = jnp.dot(
-            pick, part, preferred_element_type=jnp.float32
+        tot[pl.ds(k, rows, stride=folds), :] = lax.dot_general(
+            pick, part, (((0,), (0,)), ((), ())), preferred_element_type=jnp.float32
+        )
+    out_ref[...] = tot[...].astype(jnp.bfloat16)
+
+
+def peer_id(peer):
+    count = lax.axis_size("slide")
+    return {"seq": lax.div(peer, count), "slide": lax.rem(peer, count)}
+
+
+def greet_all(shards, me):
+    barrier = pltpu.get_barrier_semaphore()
+
+    def greet(i, _):
+        pl.semaphore_signal(
+            barrier, inc=1, device_id=peer_id(lax.rem(me + i, shards)),
+            device_id_type=pl.DeviceIdType.MESH,
+        )
+        return 0
+
+    lax.fori_loop(1, shards, greet, 0)
+    pl.semaphore_wait(barrier, shards - 1)
+
+
+def block_copy(src, dst, i, me, shards, send_sem, recv_sem):
+    peer = lax.rem(me + i, shards)
+    return pltpu.make_async_remote_copy(
+        src_ref=src.at[peer], dst_ref=dst.at[me], send_sem=send_sem.at[i],
+        recv_sem=recv_sem.at[i], device_id=peer_id(peer),
+        device_id_type=pl.DeviceIdType.MESH,
+    )
+
+
+def block_landed(src, dst, i, me, shards, send_sem, recv_sem):
+    peer = lax.rem(me + i, shards)
+    origin = lax.rem(me + shards - i, shards)
+    return pltpu.make_async_remote_copy(
+        src_ref=src.at[peer], dst_ref=dst.at[origin], send_sem=send_sem.at[i],
+        recv_sem=recv_sem.at[i], device_id=peer_id(peer),
+        device_id_type=pl.DeviceIdType.MESH,
+    )
+
+
+def start_blocks(*args):
+    src, dst, me, shards, send_sem, recv_sem = args
+
+    def go(i, _):
+        block_copy(src, dst, i, me, shards, send_sem, recv_sem).start()
+        return 0
+
+    lax.fori_loop(1, shards, go, 0)
+
+
+def await_blocks(*args):
+    src, dst, me, shards, send_sem, recv_sem = args
+
+    def stop(i, _):
+        block_landed(src, dst, i, me, shards, send_sem, recv_sem).wait()
+        return 0
+
+    lax.fori_loop(1, shards, stop, 0)
+
+
+def arrive_kernel(
+    shards, emb_ref, slots_ref, wg_ref, wi_ref,
+    inner_ref, prev_ref, next_ref, gate_ref, place_ref,
+    scr, send, got, gslot, ordered, wg, wi,
+    send_sem, recv_sem, slot_send, slot_recv, halo_send, halo_recv, load_sem,
+):
+    rows, model = emb_ref.shape
+    width = inner_ref.shape[1]
+    folds = model // LANES
+    wide = 2 * LANES
+    edge = prev_ref.shape[0]
+    me = lax.axis_index(AXES)
+    load_gate = pltpu.make_async_copy(wg_ref, wg, load_sem.at[0])
+    load_inner = pltpu.make_async_copy(wi_ref, wi, load_sem.at[1])
+    load_gate.start()
+    load_inner.start()
+    for k in range(folds):
+        scr[pl.ds(k, rows, stride=folds), :] = emb_ref[:, k * LANES : (k + 1) * LANES].astype(
+            jnp.float32
+        )
+    send[...] = scr[...].astype(jnp.bfloat16).reshape(send.shape)
+    greet_all(shards, me)
+    start_blocks(slots_ref, gslot, me, shards, slot_send, slot_recv)
+    start_blocks(send, got, me, shards, send_sem, recv_sem)
+    got[me] = send[me]
+    gslot[me] = slots_ref[me]
+    load_gate.wait()
+
+    def gate_tile(cb, _):
+        cols = pl.ds(pl.multiple_of(cb * wide, wide), wide)
+        v = jnp.dot(emb_ref[...], wg[:, cols], preferred_element_type=jnp.float32)
+        gate_ref[:, cols] = v / (1.0 + jnp.exp(-v))
+        return 0
+
+    lax.fori_loop(0, width // wide, gate_tile, 0)
+    load_inner.wait()
+    await_blocks(slots_ref, gslot, me, shards, slot_send, slot_recv)
+    await_blocks(send, got, me, shards, send_sem, recv_sem)
+    slot_row = jnp.sum(gslot[...], axis=0)
+    place = (
+        jnp.broadcast_to(slot_row, (rows, rows))
+        == lax.broadcasted_iota(jnp.int32, (rows, rows), 0).astype(jnp.float32)
+    ).astype(jnp.bfloat16)
+    place_ref[...] = place
+    scr[...] = got[...].astype(jnp.float32).reshape(scr.shape)
+    for k in range(folds):
+        ordered[:, k * LANES : (k + 1) * LANES] = jnp.dot(
+            place, scr[pl.ds(k, rows, stride=folds), :].astype(jnp.bfloat16),
+            preferred_element_type=jnp.float32,
+        ).astype(jnp.bfloat16)
+
+    def inner_tile(cb, _):
+        cols = pl.ds(pl.multiple_of(cb * wide, wide), wide)
+        inner_ref[:, cols] = jnp.dot(
+            ordered[...], wi[:, cols], preferred_element_type=jnp.float32
+        ).astype(jnp.bfloat16)
+        return 0
+
+    lax.fori_loop(0, width // wide, inner_tile, 0)
+    after = pltpu.make_async_remote_copy(
+        src_ref=inner_ref.at[pl.ds(rows - edge, edge)], dst_ref=prev_ref,
+        send_sem=halo_send.at[0], recv_sem=halo_recv.at[0],
+        device_id=peer_id(lax.rem(me + 1, shards)), device_id_type=pl.DeviceIdType.MESH,
+    )
+    before = pltpu.make_async_remote_copy(
+        src_ref=inner_ref.at[pl.ds(0, edge)], dst_ref=next_ref,
+        send_sem=halo_send.at[1], recv_sem=halo_recv.at[1],
+        device_id=peer_id(lax.rem(me + shards - 1, shards)), device_id_type=pl.DeviceIdType.MESH,
+    )
+    after.start()
+    before.start()
+    after.wait()
+    before.wait()
+
+
+def pass_kernel(
+    shards, states, rows, chunk, len_ref, pay_ref, rate_ref,
+    out_ref,
+    got, ent, send_a, recv_a, send_b, recv_b,
+):
+    depth = rate_ref.shape[0]
+    me = lax.axis_index(AXES)
+    greet_all(shards, me)
+    start_blocks(pay_ref, got, me, shards, send_a, recv_a)
+    got[me] = pay_ref[me]
+    starts = slide_starts(len_ref)
+    back = lax.div(me, states)
+    rate = rate_ref[...] * -LOG2E
+    await_blocks(pay_ref, got, me, shards, send_a, recv_a)
+    ent[...] = jnp.zeros(ent.shape, ent.dtype)
+
+    def step(i, h):
+        s = i + back * (shards - 1 - 2 * i)
+        keep = jnp.float32(1.0)
+        for c in range(rows // chunk):
+            keep = keep * keep_at(starts, s * rows + c * chunk + back * chunk)
+        ent[s, 0:depth, :] = h.astype(jnp.bfloat16)
+        blk = got[s].astype(jnp.float32)
+        return jnp.exp2(rate * blk[depth:]) * (h * keep) + blk[:depth]
+
+    lax.fori_loop(0, shards, step, jnp.zeros((depth, LANES), jnp.float32))
+    start_blocks(ent, out_ref, me, shards, send_b, recv_b)
+    out_ref[me] = ent[me]
+    await_blocks(ent, out_ref, me, shards, send_b, recv_b)
+
+
+def return_kernel(shards, back_ref, gate_ref, out_ref, got, scr, send_sem, recv_sem):
+    rows, width = out_ref.shape
+    folds = width // LANES
+    me = lax.axis_index(AXES)
+    greet_all(shards, me)
+    start_blocks(back_ref, got, me, shards, send_sem, recv_sem)
+    got[me] = back_ref[me]
+    await_blocks(back_ref, got, me, shards, send_sem, recv_sem)
+    scr[...] = got[...].astype(jnp.float32).reshape(scr.shape)
+    for k in range(folds):
+        cols = slice(k * LANES, (k + 1) * LANES)
+        out_ref[:, cols] = (
+            scr[pl.ds(k, rows, stride=folds), :] * gate_ref[:, cols]
         ).astype(jnp.bfloat16)
 
 
@@ -249,25 +429,67 @@
     smem = pl.BlockSpec(memory_space=pltpu.SMEM)
     params = pltpu.CompilerParams(vmem_limit_bytes=48 * 1024 * 1024)
 
-    slot_col = jnp.broadcast_to((destination % rows).astype(bf16)[:, None], (rows, LANES))
-    sent = jnp.concatenate([tile_embed, slot_col], axis=1).reshape(shards, per_peer, model + LANES)
-    got = lax.all_to_all(sent, AXES, split_axis=0, concat_axis=0, tiled=True)
-    got = got.reshape(rows, model + LANES)
-    slot = got[:, model].astype(jnp.int32)
-    place = (slot[None, :] == jnp.arange(rows, dtype=jnp.int32)[:, None]).astype(bf16)
-    ordered = jnp.dot(place, got[:, :model], preferred_element_type=f32).astype(bf16)
-    inner = jnp.dot(ordered, w_inner, preferred_element_type=f32).astype(bf16)
-    up = [(i, i + 1) for i in range(shards - 1)]
-    down = [(i + 1, i) for i in range(shards - 1)]
-    before = lax.ppermute(inner[rows - SUB :], AXES, up)
-    after = lax.ppermute(inner[:SUB], AXES, down)
+    any_space = pl.BlockSpec(memory_space=pl.ANY)
+    mfolds = model // LANES
+    fast = shards == 2 * states and (per_peer * mfolds) % 16 == 0 and (per_peer * folds) % 16 == 0
+    dma = pltpu.SemaphoreType.DMA((shards,))
+
+    def remote_params(number):
+        return pltpu.CompilerParams(
+            vmem_limit_bytes=48 * 1024 * 1024, collective_id=number, has_side_effects=True
+        )
+
+    if fast:
+        lane = jnp.arange(rows, dtype=jnp.int32)[None, :]
+        slots = jnp.tile((destination % rows).astype(f32).reshape(shards, per_peer), (1, shards))
+        slots = jnp.where(lane // per_peer == me, slots, 0.0)[:, None, :]
+        inner, before, after, gate, place = pl.pallas_call(
+            functools.partial(arrive_kernel, shards),
+            out_shape=(
+                jax.ShapeDtypeStruct((rows, width), bf16),
+                jax.ShapeDtypeStruct((2 * SUB, width), bf16),
+                jax.ShapeDtypeStruct((2 * SUB, width), bf16),
+                jax.ShapeDtypeStruct((rows, width), f32),
+                jax.ShapeDtypeStruct((rows, rows), bf16),
+            ),
+            in_specs=[vmem, vmem, any_space, any_space],
+            out_specs=(vmem,) * 5,
+            scratch_shapes=[
+                pltpu.VMEM((rows * mfolds, LANES), f32),
+                pltpu.VMEM((shards, per_peer * mfolds, LANES), bf16),
+                pltpu.VMEM((shards, per_peer * mfolds, LANES), bf16),
+                pltpu.VMEM((shards, 1, rows), f32),
+                pltpu.VMEM((rows, model), bf16),
+                pltpu.VMEM((model, width), bf16),
+                pltpu.VMEM((model, width), bf16),
+                dma, dma, dma, dma,
+                pltpu.SemaphoreType.DMA((2,)),
+                pltpu.SemaphoreType.DMA((2,)),
+                pltpu.SemaphoreType.DMA((2,)),
+            ],
+            compiler_params=remote_params(1),
+            name="arrive",
+        )(tile_embed, slots, w_gate, w_inner)
+    else:
+        slot_col = jnp.broadcast_to((destination % rows).astype(bf16)[:, None], (rows, LANES))
+        sent = jnp.concatenate([tile_embed, slot_col], axis=1).reshape(shards, per_peer, model + LANES)
+        got = lax.all_to_all(sent, AXES, split_axis=0, concat_axis=0, tiled=True)
+        got = got.reshape(rows, model + LANES)
+        slot = got[:, model].astype(jnp.int32)
+        place = (slot[None, :] == jnp.arange(rows, dtype=jnp.int32)[:, None]).astype(bf16)
+        ordered = jnp.dot(place, got[:, :model], preferred_element_type=f32).astype(bf16)
+        inner = jnp.dot(ordered, w_inner, preferred_element_type=f32).astype(bf16)
+        up = [(i, i + 1) for i in range(shards - 1)]
+        down = [(i + 1, i) for i in range(shards - 1)]
+        before = lax.ppermute(inner[rows - 2 * SUB :], AXES, up)
+        after = lax.ppermute(inner[: 2 * SUB], AXES, down)
     dt, proj, y, pay = pl.pallas_call(
         functools.partial(sweep_kernel, states, rank, chunk),
         out_shape=(
             jax.ShapeDtypeStruct((2, rows * folds, LANES), f32),
             jax.ShapeDtypeStruct((2 * rows, LANES), f32),
             jax.ShapeDtypeStruct((rows * folds, LANES), f32),
-            jax.ShapeDtypeStruct((2 * states, 2 * folds, LANES), f32),
+            jax.ShapeDtypeStruct((2 * states, 2 * folds, LANES), bf16),
         ),
         in_specs=[smem, smem] + [vmem] * 10,
         out_specs=(vmem,) * 4,
@@ -276,6 +498,7 @@
             pltpu.VMEM((2, rows * folds, LANES), f32),
             pltpu.VMEM((2 * states * folds, LANES), f32),
             pltpu.VMEM((rows, width), bf16),
+            pltpu.VMEM((2 * states, 2 * folds, LANES), f32),
             pltpu.SMEM((2 * rows, LANES), f32),
             pltpu.SemaphoreType.DMA,
         ],
@@ -286,25 +509,41 @@
         x_project, dt_project, dt_bias, decay.reshape(2 * states, width),
         skip_gain.reshape(2, folds, LANES),
     )
-    pay = pay.astype(bf16).reshape(2 * states, 2, split, folds // split, LANES)
-    pay = pay.swapaxes(1, 2).reshape(shards, 2 * folds // split, LANES)
-    theirs = lax.all_to_all(pay, AXES, split_axis=0, concat_axis=0, tiled=True)
-    my_rate = lax.dynamic_slice_in_dim(
-        decay.reshape(shards, folds // split, LANES), me, 1, axis=0
-    )[0]
-    enter = pl.pallas_call(
-        functools.partial(relay_kernel, states, split, rows, chunk),
-        out_shape=jax.ShapeDtypeStruct((shards, folds // split, LANES), bf16),
-        in_specs=[smem, smem, vmem, vmem],
-        out_specs=vmem,
-        compiler_params=params,
-        name="relay",
-    )(me_arr, slide_lengths, theirs, my_rate)
-    enter = lax.all_to_all(enter, AXES, split_axis=0, concat_axis=0, tiled=True)
-    enter = enter.reshape(2 * states, folds, LANES)
+    if fast:
+        my_rate = lax.dynamic_index_in_dim(decay.reshape(shards, width), me, 0, keepdims=False)
+        enter = pl.pallas_call(
+            functools.partial(pass_kernel, shards, states, rows, chunk),
+            out_shape=jax.ShapeDtypeStruct((shards, 32, LANES), bf16),
+            in_specs=[smem, vmem, vmem],
+            out_specs=vmem,
+            scratch_shapes=[
+                pltpu.VMEM((shards, 2 * folds, LANES), bf16),
+                pltpu.VMEM((shards, 32, LANES), bf16),
+                dma, dma, dma, dma,
+            ],
+            compiler_params=remote_params(2),
+            name="relay",
+        )(slide_lengths, pay, my_rate.reshape(folds, LANES))
+    else:
+        pay = pay.reshape(2 * states, 2, split, folds // split, LANES)
+        pay = pay.swapaxes(1, 2).reshape(shards, 2 * folds // split, LANES)
+        theirs = lax.all_to_all(pay, AXES, split_axis=0, concat_axis=0, tiled=True)
+        my_rate = lax.dynamic_slice_in_dim(
+            decay.reshape(shards, folds // split, LANES), me, 1, axis=0
+        )[0]
+        enter = pl.pallas_call(
+            functools.partial(relay_kernel, states, split, rows, chunk),
+            out_shape=jax.ShapeDtypeStruct((shards, folds // split, LANES), bf16),
+            in_specs=[smem, smem, vmem, vmem],
+            out_specs=vmem,
+            compiler_params=params,
+            name="relay",
+        )(me_arr, slide_lengths, theirs, my_rate)
+        enter = lax.all_to_all(enter, AXES, split_axis=0, concat_axis=0, tiled=True)
+        enter = enter.reshape(2 * states, folds, LANES)
     back = pl.pallas_call(
         functools.partial(finish_kernel, states, rank, chunk),
-        out_shape=jax.ShapeDtypeStruct((rows, width), bf16),
+        out_shape=jax.ShapeDtypeStruct((rows * folds, LANES), bf16),
         in_specs=[smem, smem, smem] + [vmem] * 5,
         out_specs=vmem,
         scratch_shapes=[
@@ -315,8 +554,22 @@
         name="finish",
     )(
         me_arr, slide_lengths, proj, dt, y, enter, decay.reshape(2 * states, width),
-        slot[:, None],
-    )
+        place,
+    )
+    if fast:
+        return pl.pallas_call(
+            functools.partial(return_kernel, shards),
+            out_shape=jax.ShapeDtypeStruct((rows, width), bf16),
+            in_specs=[vmem, vmem],
+            out_specs=vmem,
+            scratch_shapes=[
+                pltpu.VMEM((shards, per_peer * folds, LANES), bf16),
+                pltpu.VMEM((rows * folds, LANES), f32),
+                dma, dma,
+            ],
+            compiler_params=remote_params(3),
+            name="giveback",
+        )(back.reshape(shards, per_peer * folds, LANES), gate)
     back = back.reshape(shards, per_peer, width)
     returned = lax.all_to_all(back, AXES, split_axis=0, concat_axis=0, tiled=True)
     gate = jnp.dot(tile_embed, w_gate, preferred_element_type=f32)

time: 150 us -> 141 us (0.940)
  the two profiles are of different devices: /device:TPU:0 before, /device:TPU:15 now
where the time goes in v2:
time: 141 us
  Pallas kernels  124 us (88%)
  local copies, waits for them, and re-layouts  16.2 us (11%)
    pallas_call x1, Pallas kernels, local(): pl.pallas_call(functools.partial(sweep_kernel, states, rank, chunk), out_...  32.1 us
    pallas_call x1, Pallas kernels, local(): pl.pallas_call(functools.partial(pass_kernel, shards, states, rows, chunk...  25.9 us
    pallas_call x1, Pallas kernels, local(): pl.pallas_call(functools.partial(return_kernel, shards), out_shape=jax.Sh...  25.1 us
    pallas_call x1, Pallas kernels, local(): pl.pallas_call(functools.partial(arrive_kernel, shards), out_shape=(jax.S...  22.4 us
    pallas_call x1, Pallas kernels, local(): pl.pallas_call(functools.partial(finish_kernel, states, rank, chunk), out...  18.2 us
    unnamed x44, local copies, waits for them, and re-layouts  15.2 us

profile of v2, /device:TPU:15, one launch (start us, length us, event | category | flops | bytes accessed | tf_op | source)
XLA Modules:
  0.0 140.7 jit_solution(11345507970787067168)
XLA Ops:
  0.0 0.7 fusion.1
  0.7 0.1 tile.10
  0.8 0.1 copy.13
  0.9 0.1 copy.14
  1.0 0.0 copy-start.7
  1.0 1.0 copy-done.7
  2.0 0.0 copy-start.19
  2.0 0.0 copy-start.20
  2.0 0.0 copy-start
  2.0 0.0 copy-start.18
  2.0 22.4 %arrive.1 = (bf16[128,3072]{1,0:T(8,128)(2,1)S(1)}, bf16[16,3072]{1,0:T(8,128)(2,1)S(1)}, bf16[16,3072]{1,0:T(8,128)(2,1)S(1)}, f32[128,3072]{1,0:T(8,128)S(1)}, bf16[128,128]{1,0:T(8,128)(2,1)S(1)}) custom-call(bf16[128,1536]{1,0:T(8,128)(2,1)S(1)} %copy-done.7, f32[32,1,128]{2,1,0:T(1,128)S(1)} %broadcast_select_fusion.slots_ref, ...), custom_call_target="tpu_custom_call" | custom-call | tf_op jit(solution)/shard_map/arrive/pallas_call | solution.py:446
  24.4 0.0 copy-start.2
  24.4 0.9 copy-done.2
  25.2 0.0 copy-start.10
  25.2 0.6 copy-done.10
  25.9 0.0 copy-start.12
  25.9 0.6 copy-done.12
  26.5 0.0 copy-start.14
  26.5 0.6 copy-done.14
  27.1 0.0 copy-done.19
  27.1 0.7 reshape.91.cw_ref
  27.8 0.0 copy-done.20
  27.8 0.0 copy-done
  27.8 0.0 copy-done.18
  27.8 0.0 copy-start.1
  27.8 1.3 copy-done.1
  29.1 1.1 copy-done.3
  30.2 0.0 copy-start.6
  30.2 0.9 copy-done.6
  31.1 0.0 copy-start.11
  31.1 0.9 copy-done.11
  32.0 0.9 copy-done.13
  32.9 0.0 copy-start.16
  32.9 0.7 copy-done.16
  33.7 0.7 copy-done.17
  34.4 32.1 %sweep.1 = (f32[2,3072,128]{2,1,0:T(8,128)}, f32[256,128]{1,0:T(8,128)S(1)}, f32[3072,128]{1,0:T(8,128)S(1)}, bf16[32,48,128]{2,1,0:T(8,128)(2,1)S(1)}) custom-call(s32[1]{0:T(128)} %bitcast.me_ref, s32[4]{0:T(128)S(1)} %copy-done.18, bf16[128,3072]{1,0:T(8,128)(2,1)S(1)} %copy-done.3, bf16[16,3072]{1,0:T(8,128)(2,1)S(1)} %copy-done.11, ...), custom_call_target="tpu_custom_call" | custom-call | tf_op jit(solution)/shard_map/sweep/pallas_call | solution.py:486
  66.5 0.0 copy-start.4
  66.5 0.7 copy-done.4
  67.2 0.6 copy-done.8
  67.9 0.0 copy-start.5
  67.9 1.0 copy-done.5
  68.9 25.9 %relay.1.enter_ref = bf16[32,32,128]{2,1,0:T(8,128)(2,1)S(1)} custom-call(s32[4]{0:T(128)S(1)} %copy-done.18, bf16[32,48,128]{2,1,0:T(8,128)(2,1)S(1)} %copy-done.5, f32[24,128]{1,0:T(8,128)S(1)} %bitcast.14), custom_call_target="tpu_custom_call" | custom-call | tf_op jit(solution)/shard_map/relay/pallas_call | solution.py:514
  94.8 0.0 copy-start.9
  94.8 0.9 copy-done.9
  95.7 0.8 copy-done.15
  96.5 18.2 %finish.1 = bf16[3072,128]{1,0:T(8,128)(2,1)S(1)} custom-call(s32[1]{0:T(128)} %bitcast.me_ref, s32[4]{0:T(128)S(1)} %copy-done.18, f32[256,128]{1,0:T(8,128)S(1)} %copy-done.9, f32[2,3072,128]{2,1,0:T(8,128)} %get-tuple-element.18.dt_ref, f32[3072,128]{1,0:T(8,128)S(1)} %get-tuple-element.19.y_ref, bf16[32,32,128]{2,1,0:T(8,128)(2,1)S(1)} %relay.1.enter_ref, ...), custom_call_target="tpu_custom_call" | custom-call | tf_op jit(solution)/shard_map/finish/pallas_call | solution.py:544
  114.7 25.1 %giveback.1 = bf16[128,3072]{1,0:T(8,128)(2,1)S(1)} custom-call(bf16[32,96,128]{2,1,0:T(8,128)(2,1)S(1)} %bitcast.9, f32[128,3072]{1,0:T(8,128)S(1)} %get-tuple-element.22.gate_ref), custom_call_target="tpu_custom_call" | custom-call | tf_op jit(solution)/shard_map/giveback/pallas_call | solution.py:560
  139.8 0.9 copy.19
  (10 shorter events, 0.1 us)
Async XLA Ops:
  1.0 1.0 copy-start.7
  2.0 25.2 %copy-start.19 = (f32[2,4,3072]{2,1,0:T(4,128)S(1)}, f32[2,4,3072]{2,1,0:T(4,128)}, u32[]{:S(2)}) copy-start(f32[2,4,3072]{2,1,0:T(4,128)} %param.17) | copy-start | bytes 294916
  2.0 25.8 %copy-start.20 = (f32[2,3072]{1,0:T(2,128)S(1)}, f32[2,3072]{1,0:T(2,128)}, u32[]{:S(2)}) copy-start(f32[2,3072]{1,0:T(2,128)} %param.23) | copy-start | bytes 73732
  2.0 25.8 %copy-start = (f32[2,16,3072]{2,1,0:T(8,128)S(1)}, f32[2,16,3072]{2,1,0:T(8,128)}, u32[]{:S(2)}) copy-start(f32[2,16,3072]{2,1,0:T(8,128)} %param.22) | copy-start | bytes 1179652
  2.0 25.8 %copy-start.18 = (s32[4]{0:T(128)S(1)}, s32[4]{0:T(128)}, u32[]{:S(2)}) copy-start(s32[4]{0:T(128)} %len_ref.5) | copy-start | bytes 52
  24.4 0.9 copy-start.2
  25.2 0.6 copy-start.10
  25.9 0.6 copy-start.12
  26.5 0.6 copy-start.14
  27.8 1.3 copy-start.1
  29.1 1.1 copy-start.3
  30.2 0.9 copy-start.6
  31.1 0.9 copy-start.11
  32.0 0.9 copy-start.13
  32.9 0.7 copy-start.16
  33.7 0.7 copy-start.17
  66.5 0.7 copy-start.4
  67.2 0.6 copy-start.8
  67.9 1.0 copy-start.5
  94.8 0.9 copy-start.9
  95.7 0.8 copy-start.15

commit v3 on v2

--- a/solution.py
+++ b/solution.py
@@ -35,19 +35,14 @@
         )
 
 
-def sweep_kernel(
-    states, rank, chunk,
-    me_ref, len_ref, inner_ref, prev_ref, next_ref, cw_ref, cb_ref, xp_ref, dp_ref, db_ref,
-    decay_ref, skip_ref,
-    dt_ref, proj_ref, y_ref, pay_ref,
-    pad, u_ref, rate_scr, ubf, held, bc, sem,
+def prepare(
+    rank, starts, base, inner_ref, prev_ref, next_ref, cw_ref, cb_ref, xp_ref, dp_ref, db_ref,
+    decay_ref, dt_ref, proj_ref, pad, u_ref, rate_scr, ubf, bc, sem,
 ):
     rows, width = inner_ref.shape
     folds = width // LANES
     taps = cw_ref.shape[0] // 2
     halo = prev_ref.shape[0]
-    starts = slide_starts(len_ref)
-    base = me_ref[0] * rows
     spread_rates(decay_ref, rate_scr, folds)
     pad[0:SUB, :] = prev_ref[halo - SUB :, :].astype(jnp.float32)
     pad[SUB : SUB + rows, :] = inner_ref[...].astype(jnp.float32)
@@ -99,9 +94,12 @@
     copy = pltpu.make_async_copy(proj_ref, bc, sem)
     copy.start()
     copy.wait()
+
+
+def sweep_one(d, states, rank, chunk, rows, folds, starts, base, rate_scr, skip_ref, dt_ref, u_ref, bc, y_ref, keep_last):
     chunks = rows // chunk
     zero = jnp.zeros((SUB, LANES), jnp.float32)
-    for d in range(2):
+    if True:
         for j in range(folds // SUB):
             rates = [
                 rate_scr[(d * states + n) * folds + j * SUB : (d * states + n) * folds + (j + 1) * SUB, :]
@@ -140,9 +138,35 @@
                 return lax.fori_loop(0, chunk, row_step, (hs, sdt), unroll=2)
 
             hs, sdt = lax.fori_loop(0, chunks, chunk_step, ((zero,) * states, zero))
+            keep_last(j, hs, sdt)
+
+
+def sweep_kernel(
+    states, rank, chunk,
+    me_ref, len_ref, inner_ref, prev_ref, next_ref, cw_ref, cb_ref, xp_ref, dp_ref, db_ref,
+    decay_ref, skip_ref,
+    dt_ref, proj_ref, y_ref, pay_ref,
+    pad, u_ref, rate_scr, ubf, held, bc, sem,
+):
+    rows, width = inner_ref.shape
+    folds = width // LANES
+    starts = slide_starts(len_ref)
+    base = me_ref[0] * rows
+    prepare(
+        rank, starts, base, inner_ref, prev_ref, next_ref, cw_ref, cb_ref, xp_ref, dp_ref, db_ref,
+        decay_ref, dt_ref, proj_ref, pad, u_ref, rate_scr, ubf, bc, sem,
+    )
+    for d in range(2):
+
+        def keep_last(j, hs, sdt):
             for n in range(states):
                 held[d * states + n, j * SUB : (j + 1) * SUB, :] = hs[n]
                 held[d * states + n, folds + j * SUB : folds + (j + 1) * SUB, :] = sdt
+
+        sweep_one(
+            d, states, rank, chunk, rows, folds, starts, base, rate_scr, skip_ref, dt_ref, u_ref,
+            bc, y_ref, keep_last,
+        )
     pay_ref[...] = held[...].astype(jnp.bfloat16)
 
 
@@ -167,6 +191,47 @@
     lax.fori_loop(0, shards, step, jnp.zeros((depth, LANES), jnp.float32))
 
 
+def finish_one(d, j, states, rank, chunk, rows, folds, starts, base, rate_scr, enter_of, dt_ref, bc, y_ref, tot):
+    chunks = rows // chunk
+    rates = [
+        rate_scr[(d * states + n) * folds + j * SUB : (d * states + n) * folds + (j + 1) * SUB, :]
+        for n in range(states)
+    ]
+    enters = [
+        enter_of(n)
+        for n in range(states)
+    ]
+
+    def chunk_step(ci, carry):
+        alive, sdt = carry
+        c = ci if d == 0 else chunks - 1 - ci
+        alive = alive * keep_at(starts, base + (c if d == 0 else c + 1) * chunk)
+
+        def row_step(i, sdt):
+            t = c * chunk + (i if d == 0 else chunk - 1 - i)
+            spot = pl.ds(pl.multiple_of(t * folds + j * SUB, SUB), SUB)
+            sdt = sdt + dt_ref[d, spot, :]
+            parts = [None] * 4
+            for n in range(states):
+                term = jnp.exp2(sdt * rates[n]) * (
+                    enters[n] * bc[d * rows + t, rank + states + n]
+                )
+                q = n % 4
+                parts[q] = term if parts[q] is None else parts[q] + term
+            y = ((parts[0] + parts[1]) + (parts[2] + parts[3])) * alive
+            if d == 0:
+                tot[spot, :] = y_ref[spot, :] + y
+            else:
+                tot[spot, :] += y
+            return sdt
+
+        return (alive, lax.fori_loop(0, chunk, row_step, sdt, unroll=2))
+
+    lax.fori_loop(
+        0, chunks, chunk_step, (jnp.float32(1.0), jnp.zeros((SUB, LANES), jnp.float32))
+    )
+
+
 def finish_kernel(
     states, rank, chunk,
     me_ref, len_ref, bc, dt_ref, y_ref, enter_ref, decay_ref, place_ref,
@@ -175,48 +240,18 @@
 ):
     rows = place_ref.shape[0]
     folds = decay_ref.shape[1] // LANES
-    chunks = rows // chunk
     starts = slide_starts(len_ref)
     base = me_ref[0] * rows
     spread_rates(decay_ref, rate_scr, folds)
     for d in range(2):
         for j in range(folds // SUB):
-            rates = [
-                rate_scr[(d * states + n) * folds + j * SUB : (d * states + n) * folds + (j + 1) * SUB, :]
-                for n in range(states)
-            ]
-            enters = [
-                enter_ref[d * states + n, j * SUB : (j + 1) * SUB, :].astype(jnp.float32)
-                for n in range(states)
-            ]
-
-            def chunk_step(ci, carry):
-                alive, sdt = carry
-                c = ci if d == 0 else chunks - 1 - ci
-                alive = alive * keep_at(starts, base + (c if d == 0 else c + 1) * chunk)
-
-                def row_step(i, sdt):
-                    t = c * chunk + (i if d == 0 else chunk - 1 - i)
-                    spot = pl.ds(pl.multiple_of(t * folds + j * SUB, SUB), SUB)
-                    sdt = sdt + dt_ref[d, spot, :]
-                    parts = [None] * 4
-                    for n in range(states):
-                        term = jnp.exp2(sdt * rates[n]) * (
-                            enters[n] * bc[d * rows + t, rank + states + n]
-                        )
-                        q = n % 4
-                        parts[q] = term if parts[q] is None else parts[q] + term
-                    y = ((parts[0] + parts[1]) + (parts[2] + parts[3])) * alive
-                    if d == 0:
-                        tot[spot, :] = y_ref[spot, :] + y
-                    else:
-                        tot[spot, :] += y
-                    return sdt
-
-                return (alive, lax.fori_loop(0, chunk, row_step, sdt, unroll=2))
-
-            lax.fori_loop(
-                0, chunks, chunk_step, (jnp.float32(1.0), jnp.zeros((SUB, LANES), jnp.float32))
+
+            def enter_of(n):
+                return enter_ref[d * states + n, j * SUB : (j + 1) * SUB, :].astype(jnp.float32)
+
+            finish_one(
+                d, j, states, rank, chunk, rows, folds, starts, base, rate_scr, enter_of, dt_ref,
+                bc, y_ref, tot,
             )
     pick = place_ref[...]
     for k in range(folds):
@@ -243,7 +278,10 @@
         return 0
 
     lax.fori_loop(1, shards, greet, 0)
-    pl.semaphore_wait(barrier, shards - 1)
+
+
+def await_all(shards):
+    pl.semaphore_wait(pltpu.get_barrier_semaphore(), shards - 1)
 
 
 def block_copy(src, dst, i, me, shards, send_sem, recv_sem):
@@ -299,6 +337,7 @@
     me = lax.axis_index(AXES)
     load_gate = pltpu.make_async_copy(wg_ref, wg, load_sem.at[0])
     load_inner = pltpu.make_async_copy(wi_ref, wi, load_sem.at[1])
+    greet_all(shards, me)
     load_gate.start()
     load_inner.start()
     for k in range(folds):
@@ -306,7 +345,7 @@
             jnp.float32
         )
     send[...] = scr[...].astype(jnp.bfloat16).reshape(send.shape)
-    greet_all(shards, me)
+    await_all(shards)
     start_blocks(slots_ref, gslot, me, shards, slot_send, slot_recv)
     start_blocks(send, got, me, shards, send_sem, recv_sem)
     got[me] = send[me]
@@ -360,51 +399,131 @@
     before.wait()
 
 
-def pass_kernel(
-    shards, states, rows, chunk, len_ref, pay_ref, rate_ref,
+def layer_kernel(
+    shards, states, rank, chunk, groups,
+    len_ref, inner_ref, prev_ref, next_ref, cw_ref, cb_ref, xp_ref, dp_ref, db_ref, decay_ref,
+    skip_ref, myrate_ref, place_ref, gate_ref,
     out_ref,
-    got, ent, send_a, recv_a, send_b, recv_b,
+    dt_ref, proj_ref, y_ref, pad, u_ref, rate_scr, ubf, held, bc, sem,
+    stage, gotf, passes, pay0, pay1, got0, got1, ent0, ent1, land0, land1, enters,
+    turn, back0, back1, back2, home0, home1, home2, send_sem, recv_sem,
 ):
-    depth = rate_ref.shape[0]
+    rows, width = inner_ref.shape
+    folds = width // LANES
+    per = folds // groups
+    quads = shards // groups
+    some = states // quads
+    tall = some * per
     me = lax.axis_index(AXES)
+    pays, gots, ents, lands = (pay0, pay1), (got0, got1), (ent0, ent1), (land0, land1)
+    backs, homes = (back0, back1, back2), (home0, home1, home2)
+    f32, bf16 = jnp.float32, jnp.bfloat16
+
+    def route(src, dst, number):
+        return (src, dst, me, shards, send_sem.at[number], recv_sem.at[number])
+
     greet_all(shards, me)
-    start_blocks(pay_ref, got, me, shards, send_a, recv_a)
-    got[me] = pay_ref[me]
     starts = slide_starts(len_ref)
-    back = lax.div(me, states)
-    rate = rate_ref[...] * -LOG2E
-    await_blocks(pay_ref, got, me, shards, send_a, recv_a)
-    ent[...] = jnp.zeros(ent.shape, ent.dtype)
-
-    def step(i, h):
-        s = i + back * (shards - 1 - 2 * i)
-        keep = jnp.float32(1.0)
-        for c in range(rows // chunk):
-            keep = keep * keep_at(starts, s * rows + c * chunk + back * chunk)
-        ent[s, 0:depth, :] = h.astype(jnp.bfloat16)
-        blk = got[s].astype(jnp.float32)
-        return jnp.exp2(rate * blk[depth:]) * (h * keep) + blk[:depth]
-
-    lax.fori_loop(0, shards, step, jnp.zeros((depth, LANES), jnp.float32))
-    start_blocks(ent, out_ref, me, shards, send_b, recv_b)
-    out_ref[me] = ent[me]
-    await_blocks(ent, out_ref, me, shards, send_b, recv_b)
-
-
-def return_kernel(shards, back_ref, gate_ref, out_ref, got, scr, send_sem, recv_sem):
-    rows, width = out_ref.shape
-    folds = width // LANES
-    me = lax.axis_index(AXES)
-    greet_all(shards, me)
-    start_blocks(back_ref, got, me, shards, send_sem, recv_sem)
-    got[me] = back_ref[me]
-    await_blocks(back_ref, got, me, shards, send_sem, recv_sem)
-    scr[...] = got[...].astype(jnp.float32).reshape(scr.shape)
-    for k in range(folds):
-        cols = slice(k * LANES, (k + 1) * LANES)
-        out_ref[:, cols] = (
-            scr[pl.ds(k, rows, stride=folds), :] * gate_ref[:, cols]
-        ).astype(jnp.bfloat16)
+    base = me * rows
+    prepare(
+        rank, starts, base, inner_ref, prev_ref, next_ref, cw_ref, cb_ref, xp_ref, dp_ref, db_ref,
+        decay_ref, dt_ref, proj_ref, pad, u_ref, rate_scr, ubf, bc, sem,
+    )
+    stage[...] = jnp.zeros(stage.shape, f32)
+    passes[...] = jnp.zeros(passes.shape, f32)
+
+    def keep_last(j, hs, sdt):
+        for n in range(states):
+            held[n * folds + j * SUB : n * folds + (j + 1) * SUB, :] = hs[n]
+        held[states * folds + j * SUB : states * folds + (j + 1) * SUB, :] = sdt
+
+    def sweep(d):
+        sweep_one(
+            d, states, rank, chunk, rows, folds, starts, base, rate_scr, skip_ref, dt_ref, u_ref,
+            bc, y_ref, keep_last,
+        )
+        for g in range(groups):
+            for q in range(quads):
+                spot = (g * quads + q) * 2 * SUB
+                for m in range(some):
+                    row = (q * some + m) * folds + g * per
+                    stage[spot + m * per : spot + (m + 1) * per, :] = held[row : row + per, :]
+                row = states * folds + g * per
+                stage[spot + tall : spot + tall + per, :] = held[row : row + per, :]
+        pays[d][...] = stage[...].astype(bf16).reshape(pays[d].shape)
+
+    def launch(d):
+        start_blocks(*route(pays[d], gots[d], d))
+        gots[d][me] = pays[d][me]
+
+    def relay(d):
+        await_blocks(*route(pays[d], gots[d], d))
+        gotf[...] = gots[d][...].astype(f32)
+        for m in range(some):
+            rate = myrate_ref[d, m * per : (m + 1) * per, :] * -LOG2E
+            passes[:, m * per : (m + 1) * per, :] = jnp.exp2(
+                rate[None] * gotf[:, tall : tall + per, :]
+            )
+
+        def step(i, h):
+            s = i if d == 0 else shards - 1 - i
+            keep = jnp.float32(1.0)
+            for c in range(rows // chunk):
+                keep = keep * keep_at(starts, s * rows + c * chunk + d * chunk)
+            ents[d][s] = h.astype(bf16)
+            return passes[s] * (h * keep) + gotf[s]
+
+        lax.fori_loop(0, shards, step, jnp.zeros((2 * SUB, LANES), f32))
+        start_blocks(*route(ents[d], lands[d], 2 + d))
+        lands[d][me] = ents[d][me]
+
+    def arrive(d):
+        await_blocks(*route(ents[d], lands[d], 2 + d))
+        gotf[...] = lands[d][...].astype(f32)
+        for g in range(groups):
+            for q in range(quads):
+                for m in range(some):
+                    row = (q * some + m) * folds + g * per
+                    enters[row : row + per, :] = gotf[g * quads + q, m * per : (m + 1) * per, :]
+
+    def finish(d, j):
+        def enter_of(n):
+            return enters[n * folds + j * SUB : n * folds + (j + 1) * SUB, :]
+
+        finish_one(
+            d, j, states, rank, chunk, rows, folds, starts, base, rate_scr, enter_of, dt_ref, bc,
+            y_ref, y_ref,
+        )
+
+    sweep(0)
+    await_all(shards)
+    launch(0)
+    sweep(1)
+    relay(0)
+    launch(1)
+    arrive(0)
+    for j in range(folds // SUB):
+        finish(0, j)
+    relay(1)
+    arrive(1)
+    for j in range(folds // SUB):
+        finish(1, j)
+        for k in range(SUB):
+            part = y_ref[pl.ds(j * SUB + k, rows, stride=folds), :].astype(bf16)
+            turn[pl.ds(k, rows, stride=SUB), :] = lax.dot_general(
+                place_ref[...], part, (((0,), (0,)), ((), ())), preferred_element_type=f32
+            )
+        backs[j][...] = turn[...].astype(bf16).reshape(backs[j].shape)
+        start_blocks(*route(backs[j], homes[j], 4 + j))
+        homes[j][me] = backs[j][me]
+    for j in range(folds // SUB):
+        await_blocks(*route(backs[j], homes[j], 4 + j))
+        turn[...] = homes[j][...].astype(f32).reshape(turn.shape)
+        for k in range(SUB):
+            cols = slice((j * SUB + k) * LANES, (j * SUB + k + 1) * LANES)
+            out_ref[:, cols] = (
+                turn[pl.ds(k, rows, stride=SUB), :] * gate_ref[:, cols]
+            ).astype(bf16)
 
 
 def local(
@@ -427,16 +546,21 @@
     f32, bf16 = jnp.float32, jnp.bfloat16
     vmem = pl.BlockSpec(memory_space=pltpu.VMEM)
     smem = pl.BlockSpec(memory_space=pltpu.SMEM)
-    params = pltpu.CompilerParams(vmem_limit_bytes=48 * 1024 * 1024)
+    params = pltpu.CompilerParams(vmem_limit_bytes=60 * 1024 * 1024)
 
     any_space = pl.BlockSpec(memory_space=pl.ANY)
     mfolds = model // LANES
-    fast = shards == 2 * states and (per_peer * mfolds) % 16 == 0 and (per_peer * folds) % 16 == 0
+    groups = 8
+    fast = (
+        shards == 2 * states and shards % groups == 0 and folds == 3 * SUB
+        and states % (shards // groups) == 0 and (per_peer * mfolds) % 16 == 0
+        and (per_peer * SUB) % 16 == 0
+    )
     dma = pltpu.SemaphoreType.DMA((shards,))
 
     def remote_params(number):
         return pltpu.CompilerParams(
-            vmem_limit_bytes=48 * 1024 * 1024, collective_id=number, has_side_effects=True
+            vmem_limit_bytes=60 * 1024 * 1024, collective_id=number, has_side_effects=True
         )
 
     if fast:
@@ -483,6 +607,47 @@
         down = [(i + 1, i) for i in range(shards - 1)]
         before = lax.ppermute(inner[rows - 2 * SUB :], AXES, up)
         after = lax.ppermute(inner[: 2 * SUB], AXES, down)
+    if fast:
+        quads = shards // groups
+        mine = decay.reshape(2, quads, states // quads, groups, width // groups)
+        mine = lax.dynamic_slice_in_dim(mine, lax.rem(me, quads), 1, axis=1)
+        mine = lax.dynamic_slice_in_dim(mine, lax.div(me, quads), 1, axis=3)
+        mine = mine.reshape(2, states // quads * (folds // groups), LANES)
+        cell = pltpu.VMEM((shards, 2 * SUB, LANES), bf16)
+        third = pltpu.VMEM((shards, per_peer * SUB, LANES), bf16)
+        return pl.pallas_call(
+            functools.partial(layer_kernel, shards, states, rank, chunk, groups),
+            out_shape=jax.ShapeDtypeStruct((rows, width), bf16),
+            in_specs=[smem] + [vmem] * 13,
+            out_specs=vmem,
+            scratch_shapes=[
+                pltpu.VMEM((2, rows * folds, LANES), f32),
+                pltpu.VMEM((2 * rows, LANES), f32),
+                pltpu.VMEM((rows * folds, LANES), f32),
+                pltpu.VMEM((rows + 2 * SUB, width), f32),
+                pltpu.VMEM((2, rows * folds, LANES), f32),
+                pltpu.VMEM((2 * states * folds, LANES), f32),
+                pltpu.VMEM((rows, width), bf16),
+                pltpu.VMEM(((states + 1) * folds, LANES), f32),
+                pltpu.SMEM((2 * rows, LANES), f32),
+                pltpu.SemaphoreType.DMA,
+                pltpu.VMEM((shards * 2 * SUB, LANES), f32),
+                pltpu.VMEM((shards, 2 * SUB, LANES), f32),
+                pltpu.VMEM((shards, 2 * SUB, LANES), f32),
+                cell, cell, cell, cell, cell, cell, cell, cell,
+                pltpu.VMEM((states * folds, LANES), f32),
+                pltpu.VMEM((rows * SUB, LANES), f32),
+                third, third, third, third, third, third,
+                pltpu.SemaphoreType.DMA((7, shards)),
+                pltpu.SemaphoreType.DMA((7, shards)),
+            ],
+            compiler_params=remote_params(2),
+            name="layer",
+        )(
+            slide_lengths, inner, before, after, conv_weight.reshape(2 * taps, width), conv_bias,
+            x_project, dt_project, dt_bias, decay.reshape(2 * states, width),
+            skip_gain.reshape(2, folds, LANES), mine, place, gate,
+        )
     dt, proj, y, pay = pl.pallas_call(
         functools.partial(sweep_kernel, states, rank, chunk),
         out_shape=(
@@ -509,38 +674,22 @@
         x_project, dt_project, dt_bias, decay.reshape(2 * states, width),
         skip_gain.reshape(2, folds, LANES),
     )
-    if fast:
-        my_rate = lax.dynamic_index_in_dim(decay.reshape(shards, width), me, 0, keepdims=False)
-        enter = pl.pallas_call(
-            functools.partial(pass_kernel, shards, states, rows, chunk),
-            out_shape=jax.ShapeDtypeStruct((shards, 32, LANES), bf16),
-            in_specs=[smem, vmem, vmem],
-            out_specs=vmem,
-            scratch_shapes=[
-                pltpu.VMEM((shards, 2 * folds, LANES), bf16),
-                pltpu.VMEM((shards, 32, LANES), bf16),
-                dma, dma, dma, dma,
-            ],
-            compiler_params=remote_params(2),
-            name="relay",
-        )(slide_lengths, pay, my_rate.reshape(folds, LANES))
-    else:
-        pay = pay.reshape(2 * states, 2, split, folds // split, LANES)
-        pay = pay.swapaxes(1, 2).reshape(shards, 2 * folds // split, LANES)
-        theirs = lax.all_to_all(pay, AXES, split_axis=0, concat_axis=0, tiled=True)
-        my_rate = lax.dynamic_slice_in_dim(
-            decay.reshape(shards, folds // split, LANES), me, 1, axis=0
-        )[0]
-        enter = pl.pallas_call(
-            functools.partial(relay_kernel, states, split, rows, chunk),
-            out_shape=jax.ShapeDtypeStruct((shards, folds // split, LANES), bf16),
-            in_specs=[smem, smem, vmem, vmem],
-            out_specs=vmem,
-            compiler_params=params,
-            name="relay",
-        )(me_arr, slide_lengths, theirs, my_rate)
-        enter = lax.all_to_all(enter, AXES, split_axis=0, concat_axis=0, tiled=True)
-        enter = enter.reshape(2 * states, folds, LANES)
+    pay = pay.reshape(2 * states, 2, split, folds // split, LANES)
+    pay = pay.swapaxes(1, 2).reshape(shards, 2 * folds // split, LANES)
+    theirs = lax.all_to_all(pay, AXES, split_axis=0, concat_axis=0, tiled=True)
+    my_rate = lax.dynamic_slice_in_dim(
+        decay.reshape(shards, folds // split, LANES), me, 1, axis=0
+    )[0]
+    enter = pl.pallas_call(
+        functools.partial(relay_kernel, states, split, rows, chunk),
+        out_shape=jax.ShapeDtypeStruct((shards, folds // split, LANES), bf16),
+        in_specs=[smem, smem, vmem, vmem],
+        out_specs=vmem,
+        compiler_params=params,
+        name="relay",
+    )(me_arr, slide_lengths, theirs, my_rate)
+    enter = lax.all_to_all(enter, AXES, split_axis=0, concat_axis=0, tiled=True)
+    enter = enter.reshape(2 * states, folds, LANES)
     back = pl.pallas_call(
         functools.partial(finish_kernel, states, rank, chunk),
         out_shape=jax.ShapeDtypeStruct((rows * folds, LANES), bf16),
@@ -556,20 +705,6 @@
         me_arr, slide_lengths, proj, dt, y, enter, decay.reshape(2 * states, width),
         place,
     )
-    if fast:
-        return pl.pallas_call(
-            functools.partial(return_kernel, shards),
-            out_shape=jax.ShapeDtypeStruct((rows, width), bf16),
-            in_specs=[vmem, vmem],
-            out_specs=vmem,
-            scratch_shapes=[
-                pltpu.VMEM((shards, per_peer * folds, LANES), bf16),
-                pltpu.VMEM((rows * folds, LANES), f32),
-                dma, dma,
-            ],
-            compiler_params=remote_params(3),
-            name="giveback",
-        )(back.reshape(shards, per_peer * folds, LANES), gate)
     back = back.reshape(shards, per_peer, width)
     returned = lax.all_to_all(back, AXES, split_axis=0, concat_axis=0, tiled=True)
     gate = jnp.dot(tile_embed, w_gate, preferred_element_type=f32)

time: 141 us -> 117 us (0.83)
  the two profiles are of different devices: /device:TPU:15 before, /device:TPU:0 now
where the time goes in v3:
time: 117 us
  Pallas kernels  108 us (92%)
  local copies, waits for them, and re-layouts  6.92 us (6%)
  other arithmetic  1.31 us (1%)
    pallas_call x1, Pallas kernels, local(): pl.pallas_call(functools.partial(layer_kernel, shards, states, rank, chun...  77.4 us
    pallas_call x1, Pallas kernels, local(): pl.pallas_call(functools.partial(arrive_kernel, shards), out_shape=(jax.S...  31 us
    unnamed x4, local copies, waits for them, and re-layouts  4.49 us

profile of v3, /device:TPU:0, one launch (start us, length us, event | category | flops | bytes accessed | tf_op | source)
XLA Modules:
  0.0 116.7 jit_solution(10511485069105955763)
XLA Ops:
  0.0 0.7 fusion.1
  0.7 0.1 tile.10
  0.8 0.1 copy.14
  0.9 1.4 %copy.21 = f32[1,2,24,128]{3,2,1,0:T(8,128)} copy(f32[1,2,24,128]{3,1,2,0:T(2,128)} %bitcast.17) | data formatting | bytes 49152
  2.2 0.1 copy.15
  2.3 0.6 broadcast_select_fusion.slots_ref
  2.9 1.6 %reshape.88.cw_ref = f32[8,3072]{1,0:T(8,128)} reshape(f32[2,4,3072]{2,1,0:T(4,128)} %param.17) | data formatting | bytes 196608 | tf_op jit(solution)/shard_map/reshape | solution.py:647
  4.5 1.1 copy.19
  5.6 0.6 reshape.92.myrate_ref
  6.2 31.0 %arrive.1 = (bf16[128,3072]{1,0:T(8,128)(2,1)}, bf16[16,3072]{1,0:T(8,128)(2,1)}, bf16[16,3072]{1,0:T(8,128)(2,1)}, f32[128,3072]{1,0:T(8,128)}, bf16[128,128]{1,0:T(8,128)(2,1)}) custom-call(bf16[128,1536]{1,0:T(8,128)(2,1)} %emb_ref.1, f32[32,1,128]{2,1,0:T(1,128)} %broadcast_select_fusion.slots_ref, bf16[1536,3072]{1,0:T(8,128)(2,1)} %wg_ref.1, ...), custom_call_target="tpu_custom_call" | custom-call | tf_op jit(solution)/shard_map/arrive/pallas_call | solution.py:570
  37.2 77.4 %layer.1 = bf16[128,3072]{1,0:T(8,128)(2,1)} custom-call(s32[4]{0:T(128)} %len_ref.1, bf16[128,3072]{1,0:T(8,128)(2,1)} %get-tuple-element.10.inner_ref, bf16[16,3072]{1,0:T(8,128)(2,1)} %get-tuple-element.11.prev_ref, bf16[16,3072]{1,0:T(8,128)(2,1)} %get-tuple-element.12.next_ref, f32[8,3072]{1,0:T(8,128)} %reshape.88.cw_ref, f32[2,3072]{1,0:T(2,128)} %cb_ref.1, ...), custom_call_target="tpu_custom_call" | custom-call | tf_op jit(solution)/shard_map/layer/pallas_call | solution.py:618
  114.6 2.1 %copy.23 = bf16[128,3072]{1,0:T(8,128)(2,1)} copy(bf16[128,3072]{1,0:T(8,128)(2,1)} %layer.1) | data formatting | bytes 1572864
  (4 shorter events, 0.0 us)

commit v4 on v3

--- a/solution.py
+++ b/solution.py
@@ -28,22 +28,22 @@
 
 
 def spread_rates(decay_ref, rate_scr, folds):
-    count = decay_ref.shape[0]
-    for k in range(folds):
-        rate_scr[pl.ds(k, count, stride=folds), :] = (
-            decay_ref[:, k * LANES : (k + 1) * LANES] * -LOG2E
-        )
+    count = decay_ref.shape[1]
+    for d in range(2):
+        for k in range(folds):
+            rate_scr[pl.ds(d * count * folds + k, count, stride=folds), :] = (
+                decay_ref[d, :, k * LANES : (k + 1) * LANES] * -LOG2E
+            )
 
 
 def prepare(
     rank, starts, base, inner_ref, prev_ref, next_ref, cw_ref, cb_ref, xp_ref, dp_ref, db_ref,
-    decay_ref, dt_ref, proj_ref, pad, u_ref, rate_scr, ubf, bc, sem,
+    dt_ref, proj_ref, pad, u_ref, ubf, bc, sem,
 ):
     rows, width = inner_ref.shape
     folds = width // LANES
-    taps = cw_ref.shape[0] // 2
+    taps = cw_ref.shape[1]
     halo = prev_ref.shape[0]
-    spread_rates(decay_ref, rate_scr, folds)
     pad[0:SUB, :] = prev_ref[halo - SUB :, :].astype(jnp.float32)
     pad[SUB : SUB + rows, :] = inner_ref[...].astype(jnp.float32)
     pad[SUB + rows : 2 * SUB + rows, :] = next_ref[0:SUB, :].astype(jnp.float32)
@@ -72,7 +72,7 @@
                     term = pad[SUB + dist : SUB + dist + rows, cols]
                     if dist != 0:
                         term = term * masks[dist]
-                    total = total + cw_ref[d * taps + tap : d * taps + tap + 1, cols] * term
+                    total = total + cw_ref[d, tap : tap + 1, cols] * term
                 u = (total / (1.0 + jnp.exp(-total))).astype(jnp.bfloat16)
                 ubf[:, cols] = u
                 u_ref[d, pl.ds(k, rows, stride=folds), :] = u.astype(jnp.float32)
@@ -96,11 +96,11 @@
     copy.wait()
 
 
-def sweep_one(d, states, rank, chunk, rows, folds, starts, base, rate_scr, skip_ref, dt_ref, u_ref, bc, y_ref, keep_last):
+def sweep_one(d, states, rank, chunk, rows, folds, starts, base, rate_scr, skip_ref, dt_ref, u_ref, bc, y_ref, keep_last, parts_of=None):
     chunks = rows // chunk
     zero = jnp.zeros((SUB, LANES), jnp.float32)
     if True:
-        for j in range(folds // SUB):
+        for j in range(folds // SUB) if parts_of is None else parts_of:
             rates = [
                 rate_scr[(d * states + n) * folds + j * SUB : (d * states + n) * folds + (j + 1) * SUB, :]
                 for n in range(states)
@@ -152,9 +152,10 @@
     folds = width // LANES
     starts = slide_starts(len_ref)
     base = me_ref[0] * rows
+    spread_rates(decay_ref, rate_scr, folds)
     prepare(
         rank, starts, base, inner_ref, prev_ref, next_ref, cw_ref, cb_ref, xp_ref, dp_ref, db_ref,
-        decay_ref, dt_ref, proj_ref, pad, u_ref, rate_scr, ubf, bc, sem,
+        dt_ref, proj_ref, pad, u_ref, ubf, bc, sem,
     )
     for d in range(2):
 
@@ -239,7 +240,7 @@
     rate_scr, tot,
 ):
     rows = place_ref.shape[0]
-    folds = decay_ref.shape[1] // LANES
+    folds = decay_ref.shape[2] // LANES
     starts = slide_starts(len_ref)
     base = me_ref[0] * rows
     spread_rates(decay_ref, rate_scr, folds)
@@ -323,93 +324,24 @@
     lax.fori_loop(1, shards, stop, 0)
 
 
-def arrive_kernel(
-    shards, emb_ref, slots_ref, wg_ref, wi_ref,
-    inner_ref, prev_ref, next_ref, gate_ref, place_ref,
-    scr, send, got, gslot, ordered, wg, wi,
-    send_sem, recv_sem, slot_send, slot_recv, halo_send, halo_recv, load_sem,
+def layer_kernel(
+    shards, states, rank, chunk, groups,
+    len_ref, emb_ref, slots_ref, cw_ref, cb_ref, db_ref, skip_ref,
+    wg_ref, wi_ref, xp_hbm, dp_hbm, decay_hbm,
+    out_ref,
+    scr, send, got, gslot, ordered, wg, wi, xp_ref, dp_ref, decay_ref,
+    inner_ref, prev_ref, next_ref, gate_ref, place_ref, skip_scr,
+    dt_ref, proj_ref, y_ref, pad, u_ref, rate_scr, ubf, held, bc, sem,
+    stage, gotf, passes, pay0, pay1, got0, got1, ent0, ent1, land0, land1, enters0, enters1,
+    turn, back0, back1, back2, home0, home1, home2, send_sem, recv_sem, halo_send, halo_recv,
+    load_sem,
 ):
-    rows, model = emb_ref.shape
-    width = inner_ref.shape[1]
-    folds = model // LANES
+    rows, width = inner_ref.shape
+    model = emb_ref.shape[1]
+    folds = width // LANES
+    mfolds = model // LANES
     wide = 2 * LANES
     edge = prev_ref.shape[0]
-    me = lax.axis_index(AXES)
-    load_gate = pltpu.make_async_copy(wg_ref, wg, load_sem.at[0])
-    load_inner = pltpu.make_async_copy(wi_ref, wi, load_sem.at[1])
-    greet_all(shards, me)
-    load_gate.start()
-    load_inner.start()
-    for k in range(folds):
-        scr[pl.ds(k, rows, stride=folds), :] = emb_ref[:, k * LANES : (k + 1) * LANES].astype(
-            jnp.float32
-        )
-    send[...] = scr[...].astype(jnp.bfloat16).reshape(send.shape)
-    await_all(shards)
-    start_blocks(slots_ref, gslot, me, shards, slot_send, slot_recv)
-    start_blocks(send, got, me, shards, send_sem, recv_sem)
-    got[me] = send[me]
-    gslot[me] = slots_ref[me]
-    load_gate.wait()
-
-    def gate_tile(cb, _):
-        cols = pl.ds(pl.multiple_of(cb * wide, wide), wide)
-        v = jnp.dot(emb_ref[...], wg[:, cols], preferred_element_type=jnp.float32)
-        gate_ref[:, cols] = v / (1.0 + jnp.exp(-v))
-        return 0
-
-    lax.fori_loop(0, width // wide, gate_tile, 0)
-    load_inner.wait()
-    await_blocks(slots_ref, gslot, me, shards, slot_send, slot_recv)
-    await_blocks(send, got, me, shards, send_sem, recv_sem)
-    slot_row = jnp.sum(gslot[...], axis=0)
-    place = (
-        jnp.broadcast_to(slot_row, (rows, rows))
-        == lax.broadcasted_iota(jnp.int32, (rows, rows), 0).astype(jnp.float32)
-    ).astype(jnp.bfloat16)
-    place_ref[...] = place
-    scr[...] = got[...].astype(jnp.float32).reshape(scr.shape)
-    for k in range(folds):
-        ordered[:, k * LANES : (k + 1) * LANES] = jnp.dot(
-            place, scr[pl.ds(k, rows, stride=folds), :].astype(jnp.bfloat16),
-            preferred_element_type=jnp.float32,
-        ).astype(jnp.bfloat16)
-
-    def inner_tile(cb, _):
-        cols = pl.ds(pl.multiple_of(cb * wide, wide), wide)
-        inner_ref[:, cols] = jnp.dot(
-            ordered[...], wi[:, cols], preferred_element_type=jnp.float32
-        ).astype(jnp.bfloat16)
-        return 0
-
-    lax.fori_loop(0, width // wide, inner_tile, 0)
-    after = pltpu.make_async_remote_copy(
-        src_ref=inner_ref.at[pl.ds(rows - edge, edge)], dst_ref=prev_ref,
-        send_sem=halo_send.at[0], recv_sem=halo_recv.at[0],
-        device_id=peer_id(lax.rem(me + 1, shards)), device_id_type=pl.DeviceIdType.MESH,
-    )
-    before = pltpu.make_async_remote_copy(
-        src_ref=inner_ref.at[pl.ds(0, edge)], dst_ref=next_ref,
-        send_sem=halo_send.at[1], recv_sem=halo_recv.at[1],
-        device_id=peer_id(lax.rem(me + shards - 1, shards)), device_id_type=pl.DeviceIdType.MESH,
-    )
-    after.start()
-    before.start()
-    after.wait()
-    before.wait()
-
-
-def layer_kernel(
-    shards, states, rank, chunk, groups,
-    len_ref, inner_ref, prev_ref, next_ref, cw_ref, cb_ref, xp_ref, dp_ref, db_ref, decay_ref,
-    skip_ref, myrate_ref, place_ref, gate_ref,
-    out_ref,
-    dt_ref, proj_ref, y_ref, pad, u_ref, rate_scr, ubf, held, bc, sem,
-    stage, gotf, passes, pay0, pay1, got0, got1, ent0, ent1, land0, land1, enters,
-    turn, back0, back1, back2, home0, home1, home2, send_sem, recv_sem,
-):
-    rows, width = inner_ref.shape
-    folds = width // LANES
     per = folds // groups
     quads = shards // groups
     some = states // quads
@@ -417,31 +349,100 @@
     me = lax.axis_index(AXES)
     pays, gots, ents, lands = (pay0, pay1), (got0, got1), (ent0, ent1), (land0, land1)
     backs, homes = (back0, back1, back2), (home0, home1, home2)
+    enters = (enters0, enters1)
     f32, bf16 = jnp.float32, jnp.bfloat16
 
     def route(src, dst, number):
         return (src, dst, me, shards, send_sem.at[number], recv_sem.at[number])
 
     greet_all(shards, me)
+    pairs = ((wg_ref, wg), (decay_hbm, decay_ref), (wi_ref, wi), (xp_hbm, xp_ref), (dp_hbm, dp_ref))
+    loads = [
+        pltpu.make_async_copy(src, dst, load_sem.at[i]) for i, (src, dst) in enumerate(pairs)
+    ]
+    for load in loads:
+        load.start()
+    for k in range(mfolds):
+        scr[pl.ds(k, rows, stride=mfolds), :] = emb_ref[:, k * LANES : (k + 1) * LANES].astype(f32)
+    send[...] = scr[...].astype(bf16).reshape(send.shape)
+    await_all(shards)
+    start_blocks(*route(slots_ref, gslot, 7))
+    start_blocks(*route(send, got, 8))
+    got[me] = send[me]
+    gslot[me] = slots_ref[me]
     starts = slide_starts(len_ref)
     base = me * rows
+    for k in range(folds):
+        for d in range(2):
+            skip_scr[d, k : k + 1, :] = skip_ref[d : d + 1, k * LANES : (k + 1) * LANES]
+    stage[...] = jnp.zeros(stage.shape, f32)
+    passes[...] = jnp.zeros(passes.shape, f32)
+    loads[0].wait()
+
+    def gate_tile(cb, _):
+        cols = pl.ds(pl.multiple_of(cb * wide, wide), wide)
+        v = jnp.dot(emb_ref[...], wg[:, cols], preferred_element_type=f32)
+        gate_ref[:, cols] = v / (1.0 + jnp.exp(-v))
+        return 0
+
+    lax.fori_loop(0, width // wide, gate_tile, 0)
+    loads[1].wait()
+    spread_rates(decay_ref, rate_scr, folds)
+    for load in loads[2:]:
+        load.wait()
+    await_blocks(*route(slots_ref, gslot, 7))
+    await_blocks(*route(send, got, 8))
+    slot_row = jnp.sum(gslot[...], axis=0)
+    place = (
+        jnp.broadcast_to(slot_row, (rows, rows))
+        == lax.broadcasted_iota(jnp.int32, (rows, rows), 0).astype(f32)
+    ).astype(bf16)
+    place_ref[...] = place
+    scr[...] = got[...].astype(f32).reshape(scr.shape)
+    for k in range(mfolds):
+        ordered[:, k * LANES : (k + 1) * LANES] = jnp.dot(
+            place, scr[pl.ds(k, rows, stride=mfolds), :].astype(bf16), preferred_element_type=f32
+        ).astype(bf16)
+
+    def inner_tile(cb, _):
+        cols = pl.ds(pl.multiple_of(cb * wide, wide), wide)
+        inner_ref[:, cols] = jnp.dot(
+            ordered[...], wi[:, cols], preferred_element_type=f32
+        ).astype(bf16)
+        return 0
+
+    lax.fori_loop(0, width // wide, inner_tile, 0)
+    to_next = pltpu.make_async_remote_copy(
+        src_ref=inner_ref.at[pl.ds(rows - edge, edge)], dst_ref=prev_ref,
+        send_sem=halo_send.at[0], recv_sem=halo_recv.at[0],
+        device_id=peer_id(lax.rem(me + 1, shards)), device_id_type=pl.DeviceIdType.MESH,
+    )
+    to_prev = pltpu.make_async_remote_copy(
+        src_ref=inner_ref.at[pl.ds(0, edge)], dst_ref=next_ref,
+        send_sem=halo_send.at[1], recv_sem=halo_recv.at[1],
+        device_id=peer_id(lax.rem(me + shards - 1, shards)), device_id_type=pl.DeviceIdType.MESH,
+    )
+    to_next.start()
+    to_prev.start()
+    to_next.wait()
+    to_prev.wait()
     prepare(
         rank, starts, base, inner_ref, prev_ref, next_ref, cw_ref, cb_ref, xp_ref, dp_ref, db_ref,
-        decay_ref, dt_ref, proj_ref, pad, u_ref, rate_scr, ubf, bc, sem,
-    )
-    stage[...] = jnp.zeros(stage.shape, f32)
-    passes[...] = jnp.zeros(passes.shape, f32)
+        dt_ref, proj_ref, pad, u_ref, ubf, bc, sem,
+    )
 
     def keep_last(j, hs, sdt):
         for n in range(states):
             held[n * folds + j * SUB : n * folds + (j + 1) * SUB, :] = hs[n]
         held[states * folds + j * SUB : states * folds + (j + 1) * SUB, :] = sdt
 
-    def sweep(d):
+    def sweep(d, parts_of):
         sweep_one(
-            d, states, rank, chunk, rows, folds, starts, base, rate_scr, skip_ref, dt_ref, u_ref,
-            bc, y_ref, keep_last,
+            d, states, rank, chunk, rows, folds, starts, base, rate_scr, skip_scr, dt_ref, u_ref,
+            bc, y_ref, keep_last, parts_of,
         )
+
+    def pack(d):
         for g in range(groups):
             for q in range(quads):
                 spot = (g * quads + q) * 2 * SUB
@@ -460,10 +461,12 @@
         await_blocks(*route(pays[d], gots[d], d))
         gotf[...] = gots[d][...].astype(f32)
         for m in range(some):
-            rate = myrate_ref[d, m * per : (m + 1) * per, :] * -LOG2E
-            passes[:, m * per : (m + 1) * per, :] = jnp.exp2(
-                rate[None] * gotf[:, tall : tall + per, :]
-            )
+            row = (d * states + lax.rem(me, quads) * some + m) * folds + lax.div(me, quads) * per
+            for f in range(per):
+                rate = rate_scr[pl.ds(row + f, 1), :]
+                passes[:, m * per + f : m * per + f + 1, :] = jnp.exp2(
+                    rate[None] * gotf[:, tall + f : tall + f + 1, :]
+                )
 
         def step(i, h):
             s = i if d == 0 else shards - 1 - i
@@ -484,30 +487,18 @@
             for q in range(quads):
                 for m in range(some):
                     row = (q * some + m) * folds + g * per
-                    enters[row : row + per, :] = gotf[g * quads + q, m * per : (m + 1) * per, :]
+                    enters[d][row : row + per, :] = gotf[g * quads + q, m * per : (m + 1) * per, :]
 
     def finish(d, j):
         def enter_of(n):
-            return enters[n * folds + j * SUB : n * folds + (j + 1) * SUB, :]
+            return enters[d][n * folds + j * SUB : n * folds + (j + 1) * SUB, :]
 
         finish_one(
             d, j, states, rank, chunk, rows, folds, starts, base, rate_scr, enter_of, dt_ref, bc,
             y_ref, y_ref,
         )
 
-    sweep(0)
-    await_all(shards)
-    launch(0)
-    sweep(1)
-    relay(0)
-    launch(1)
-    arrive(0)
-    for j in range(folds // SUB):
-        finish(0, j)
-    relay(1)
-    arrive(1)
-    for j in range(folds // SUB):
-        finish(1, j)
+    def give(j):
         for k in range(SUB):
             part = y_ref[pl.ds(j * SUB + k, rows, stride=folds), :].astype(bf16)
             turn[pl.ds(k, rows, stride=SUB), :] = lax.dot_general(
@@ -516,6 +507,27 @@
         backs[j][...] = turn[...].astype(bf16).reshape(backs[j].shape)
         start_blocks(*route(backs[j], homes[j], 4 + j))
         homes[j][me] = backs[j][me]
+
+    sweep(0, (0, 1, 2))
+    pack(0)
+    launch(0)
+    sweep(1, (0, 1))
+    relay(0)
+    sweep(1, (2,))
+    pack(1)
+    launch(1)
+    arrive(0)
+    finish(0, 0)
+    relay(1)
+    finish(0, 1)
+    arrive(1)
+    finish(1, 0)
+    give(0)
+    finish(1, 1)
+    give(1)
+    finish(0, 2)
+    finish(1, 2)
+    give(2)
     for j in range(folds // SUB):
         await_blocks(*route(backs[j], homes[j], 4 + j))
         turn[...] = homes[j][...].astype(f32).reshape(turn.shape)
@@ -556,7 +568,6 @@
         and states % (shards // groups) == 0 and (per_peer * mfolds) % 16 == 0
         and (per_peer * SUB) % 16 == 0
     )
-    dma = pltpu.SemaphoreType.DMA((shards,))
 
     def remote_params(number):
         return pltpu.CompilerParams(
@@ -567,60 +578,30 @@
         lane = jnp.arange(rows, dtype=jnp.int32)[None, :]
         slots = jnp.tile((destination % rows).astype(f32).reshape(shards, per_peer), (1, shards))
         slots = jnp.where(lane // per_peer == me, slots, 0.0)[:, None, :]
-        inner, before, after, gate, place = pl.pallas_call(
-            functools.partial(arrive_kernel, shards),
-            out_shape=(
-                jax.ShapeDtypeStruct((rows, width), bf16),
-                jax.ShapeDtypeStruct((2 * SUB, width), bf16),
-                jax.ShapeDtypeStruct((2 * SUB, width), bf16),
-                jax.ShapeDtypeStruct((rows, width), f32),
-                jax.ShapeDtypeStruct((rows, rows), bf16),
-            ),
-            in_specs=[vmem, vmem, any_space, any_space],
-            out_specs=(vmem,) * 5,
-            scratch_shapes=[
-                pltpu.VMEM((rows * mfolds, LANES), f32),
-                pltpu.VMEM((shards, per_peer * mfolds, LANES), bf16),
-                pltpu.VMEM((shards, per_peer * mfolds, LANES), bf16),
-                pltpu.VMEM((shards, 1, rows), f32),
-                pltpu.VMEM((rows, model), bf16),
-                pltpu.VMEM((model, width), bf16),
-                pltpu.VMEM((model, width), bf16),
-                dma, dma, dma, dma,
-                pltpu.SemaphoreType.DMA((2,)),
-                pltpu.SemaphoreType.DMA((2,)),
-                pltpu.SemaphoreType.DMA((2,)),
-            ],
-            compiler_params=remote_params(1),
-            name="arrive",
-        )(tile_embed, slots, w_gate, w_inner)
-    else:
-        slot_col = jnp.broadcast_to((destination % rows).astype(bf16)[:, None], (rows, LANES))
-        sent = jnp.concatenate([tile_embed, slot_col], axis=1).reshape(shards, per_peer, model + LANES)
-        got = lax.all_to_all(sent, AXES, split_axis=0, concat_axis=0, tiled=True)
-        got = got.reshape(rows, model + LANES)
-        slot = got[:, model].astype(jnp.int32)
-        place = (slot[None, :] == jnp.arange(rows, dtype=jnp.int32)[:, None]).astype(bf16)
-        ordered = jnp.dot(place, got[:, :model], preferred_element_type=f32).astype(bf16)
-        inner = jnp.dot(ordered, w_inner, preferred_element_type=f32).astype(bf16)
-        up = [(i, i + 1) for i in range(shards - 1)]
-        down = [(i + 1, i) for i in range(shards - 1)]
-        before = lax.ppermute(inner[rows - 2 * SUB :], AXES, up)
-        after = lax.ppermute(inner[: 2 * SUB], AXES, down)
-    if fast:
-        quads = shards // groups
-        mine = decay.reshape(2, quads, states // quads, groups, width // groups)
-        mine = lax.dynamic_slice_in_dim(mine, lax.rem(me, quads), 1, axis=1)
-        mine = lax.dynamic_slice_in_dim(mine, lax.div(me, quads), 1, axis=3)
-        mine = mine.reshape(2, states // quads * (folds // groups), LANES)
+        sent_rows = pltpu.VMEM((shards, per_peer * mfolds, LANES), bf16)
         cell = pltpu.VMEM((shards, 2 * SUB, LANES), bf16)
         third = pltpu.VMEM((shards, per_peer * SUB, LANES), bf16)
         return pl.pallas_call(
             functools.partial(layer_kernel, shards, states, rank, chunk, groups),
             out_shape=jax.ShapeDtypeStruct((rows, width), bf16),
-            in_specs=[smem] + [vmem] * 13,
+            in_specs=[smem] + [vmem] * 6 + [any_space] * 5,
             out_specs=vmem,
             scratch_shapes=[
+                pltpu.VMEM((rows * mfolds, LANES), f32),
+                sent_rows, sent_rows,
+                pltpu.VMEM((shards, 1, rows), f32),
+                pltpu.VMEM((rows, model), bf16),
+                pltpu.VMEM((model, width), bf16),
+                pltpu.VMEM((model, width), bf16),
+                pltpu.VMEM(x_project.shape, bf16),
+                pltpu.VMEM(dt_project.shape, bf16),
+                pltpu.VMEM(decay.shape, f32),
+                pltpu.VMEM((rows, width), bf16),
+                pltpu.VMEM((2 * SUB, width), bf16),
+                pltpu.VMEM((2 * SUB, width), bf16),
+                pltpu.VMEM((rows, width), f32),
+                pltpu.VMEM((rows, rows), bf16),
+                pltpu.VMEM((2, folds, LANES), f32),
                 pltpu.VMEM((2, rows * folds, LANES), f32),
                 pltpu.VMEM((2 * rows, LANES), f32),
                 pltpu.VMEM((rows * folds, LANES), f32),
@@ -636,18 +617,33 @@
                 pltpu.VMEM((shards, 2 * SUB, LANES), f32),
                 cell, cell, cell, cell, cell, cell, cell, cell,
                 pltpu.VMEM((states * folds, LANES), f32),
+                pltpu.VMEM((states * folds, LANES), f32),
                 pltpu.VMEM((rows * SUB, LANES), f32),
                 third, third, third, third, third, third,
-                pltpu.SemaphoreType.DMA((7, shards)),
-                pltpu.SemaphoreType.DMA((7, shards)),
+                pltpu.SemaphoreType.DMA((9, shards)),
+                pltpu.SemaphoreType.DMA((9, shards)),
+                pltpu.SemaphoreType.DMA((2,)),
+                pltpu.SemaphoreType.DMA((2,)),
+                pltpu.SemaphoreType.DMA((5,)),
             ],
             compiler_params=remote_params(2),
             name="layer",
         )(
-            slide_lengths, inner, before, after, conv_weight.reshape(2 * taps, width), conv_bias,
-            x_project, dt_project, dt_bias, decay.reshape(2 * states, width),
-            skip_gain.reshape(2, folds, LANES), mine, place, gate,
+            slide_lengths, tile_embed, slots, conv_weight, conv_bias, dt_bias, skip_gain,
+            w_gate, w_inner, x_project, dt_project, decay,
         )
+    slot_col = jnp.broadcast_to((destination % rows).astype(bf16)[:, None], (rows, LANES))
+    sent = jnp.concatenate([tile_embed, slot_col], axis=1).reshape(shards, per_peer, model + LANES)
+    got = lax.all_to_all(sent, AXES, split_axis=0, concat_axis=0, tiled=True)
+    got = got.reshape(rows, model + LANES)
+    slot = got[:, model].astype(jnp.int32)
+    place = (slot[None, :] == jnp.arange(rows, dtype=jnp.int32)[:, None]).astype(bf16)
+    ordered = jnp.dot(place, got[:, :model], preferred_element_type=f32).astype(bf16)
+    inner = jnp.dot(ordered, w_inner, preferred_element_type=f32).astype(bf16)
+    up = [(i, i + 1) for i in range(shards - 1)]
+    down = [(i + 1, i) for i in range(shards - 1)]
+    before = lax.ppermute(inner[rows - 2 * SUB :], AXES, up)
+    after = lax.ppermute(inner[: 2 * SUB], AXES, down)
     dt, proj, y, pay = pl.pallas_call(
         functools.partial(sweep_kernel, states, rank, chunk),
         out_shape=(
@@ -670,8 +666,8 @@
         compiler_params=params,
         name="sweep",
     )(
-        me_arr, slide_lengths, inner, before, after, conv_weight.reshape(2 * taps, width), conv_bias,
-        x_project, dt_project, dt_bias, decay.reshape(2 * states, width),
+        me_arr, slide_lengths, inner, before, after, conv_weight, conv_bias,
+        x_project, dt_project, dt_bias, decay,
         skip_gain.reshape(2, folds, LANES),
     )
     pay = pay.reshape(2 * states, 2, split, folds // split, LANES)
@@ -702,7 +698,7 @@
         compiler_params=params,
         name="finish",
     )(
-        me_arr, slide_lengths, proj, dt, y, enter, decay.reshape(2 * states, width),
+        me_arr, slide_lengths, proj, dt, y, enter, decay,
         place,
     )
     back = back.reshape(shards, per_peer, width)

time: 117 us -> 101 us (0.86)
  Pallas kernels: 108 us -> 96.8 us
  local copies, waits for them, and re-layouts: 6.92 us -> 2.31 us
    pallas_call x1 -> x0, Pallas kernels: 31 us -> none  [local(): pl.pallas_call(functools.partial(arrive_kernel, shards), out_shape=(jax.S...]
    pallas_call x1, Pallas kernels: 77.4 us -> 96.8 us  [local(): pl.pallas_call(functools.partial(layer_kernel, shards, states, rank, chun...]
    unnamed x4 -> x1, local copies, waits for them, and re-layouts: 4.49 us -> 2.06 us
    reshape x2 -> x0, local copies, waits for them, and re-layouts: 2.17 us -> none  [the longest x1 1.57 us: local(): conv_weight.reshape(2 * taps, width)]
where the time goes in v4:
time: 101 us; the launch traced here: 100 us
  Pallas kernels  96.8 us (96%)
  local copies, waits for them, and re-layouts  2.31 us (2%)
  other arithmetic  1.31 us (1%)
    pallas_call x1, Pallas kernels, local(): pl.pallas_call(functools.partial(layer_kernel, shards, states, rank, chun...  96.8 us
    unnamed x1, local copies, waits for them, and re-layouts  2.06 us

profile of v4, /device:TPU:0, one launch (start us, length us, event | category | flops | bytes accessed | tf_op | source)
XLA Modules:
  0.0 100.5 jit_solution(13025118153739421838)
XLA Ops:
  0.0 0.7 fusion.1
  0.7 0.1 tile.10
  0.8 0.1 copy.13
  0.9 0.1 copy.14
  0.9 0.6 broadcast_select_fusion.slots_ref
  1.6 96.8 %layer.1 = bf16[128,3072]{1,0:T(8,128)(2,1)} custom-call(s32[4]{0:T(128)} %len_ref.1, bf16[128,1536]{1,0:T(8,128)(2,1)} %emb_ref.1, f32[32,1,128]{2,1,0:T(1,128)} %broadcast_select_fusion.slots_ref, f32[2,4,3072]{2,1,0:T(4,128)} %cw_ref.1, f32[2,3072]{1,0:T(2,128)} %cb_ref.1, f32[2,3072]{1,0:T(2,128)} %db_ref.1, f32[2,3072]{1,0:T(2,128)} %skip_ref.1, ...), custom_call_target="tpu_custom_call" | custom-call | tf_op jit(solution)/shard_map/layer/pallas_call | solution.py:584
  98.4 2.1 %copy.16 = bf16[128,3072]{1,0:T(8,128)(2,1)} copy(bf16[128,3072]{1,0:T(8,128)(2,1)} %layer.1) | data formatting | bytes 1572864
  (2 shorter events, 0.0 us)

commit v5 on v4

--- a/solution.py
+++ b/solution.py
@@ -135,7 +135,7 @@
                         y_ref[spot, :] += y
                     return (tuple(out), sdt + dt)
 
-                return lax.fori_loop(0, chunk, row_step, (hs, sdt), unroll=2)
+                return lax.fori_loop(0, chunk, row_step, (hs, sdt), unroll=8)
 
             hs, sdt = lax.fori_loop(0, chunks, chunk_step, ((zero,) * states, zero))
             keep_last(j, hs, sdt)
@@ -226,7 +226,7 @@
                 tot[spot, :] += y
             return sdt
 
-        return (alive, lax.fori_loop(0, chunk, row_step, sdt, unroll=2))
+        return (alive, lax.fori_loop(0, chunk, row_step, sdt, unroll=8))
 
     lax.fori_loop(
         0, chunks, chunk_step, (jnp.float32(1.0), jnp.zeros((SUB, LANES), jnp.float32))
@@ -285,43 +285,24 @@
     pl.semaphore_wait(pltpu.get_barrier_semaphore(), shards - 1)
 
 
-def block_copy(src, dst, i, me, shards, send_sem, recv_sem):
-    peer = lax.rem(me + i, shards)
-    return pltpu.make_async_remote_copy(
-        src_ref=src.at[peer], dst_ref=dst.at[me], send_sem=send_sem.at[i],
-        recv_sem=recv_sem.at[i], device_id=peer_id(peer),
-        device_id_type=pl.DeviceIdType.MESH,
-    )
-
-
-def block_landed(src, dst, i, me, shards, send_sem, recv_sem):
-    peer = lax.rem(me + i, shards)
-    origin = lax.rem(me + shards - i, shards)
-    return pltpu.make_async_remote_copy(
-        src_ref=src.at[peer], dst_ref=dst.at[origin], send_sem=send_sem.at[i],
-        recv_sem=recv_sem.at[i], device_id=peer_id(peer),
-        device_id_type=pl.DeviceIdType.MESH,
-    )
-
-
-def start_blocks(*args):
-    src, dst, me, shards, send_sem, recv_sem = args
-
+def start_blocks(src, dst, me, shards, send_sem, recv_sem):
     def go(i, _):
-        block_copy(src, dst, i, me, shards, send_sem, recv_sem).start()
+        peer = lax.rem(me + i, shards)
+        pltpu.make_async_remote_copy(
+            src_ref=src.at[peer], dst_ref=dst.at[me], send_sem=send_sem, recv_sem=recv_sem,
+            device_id=peer_id(peer), device_id_type=pl.DeviceIdType.MESH,
+        ).start()
         return 0
 
     lax.fori_loop(1, shards, go, 0)
 
 
-def await_blocks(*args):
-    src, dst, me, shards, send_sem, recv_sem = args
-
-    def stop(i, _):
-        block_landed(src, dst, i, me, shards, send_sem, recv_sem).wait()
-        return 0
-
-    lax.fori_loop(1, shards, stop, 0)
+def await_blocks(src, dst, me, shards, send_sem, recv_sem):
+    others = pl.ds(0, shards - 1)
+    pltpu.make_async_remote_copy(
+        src_ref=src.at[others], dst_ref=dst.at[others], send_sem=send_sem, recv_sem=recv_sem,
+        device_id=peer_id(lax.rem(me + 1, shards)), device_id_type=pl.DeviceIdType.MESH,
+    ).wait()
 
 
 def layer_kernel(
@@ -476,7 +457,7 @@
             ents[d][s] = h.astype(bf16)
             return passes[s] * (h * keep) + gotf[s]
 
-        lax.fori_loop(0, shards, step, jnp.zeros((2 * SUB, LANES), f32))
+        lax.fori_loop(0, shards, step, jnp.zeros((2 * SUB, LANES), f32), unroll=4)
         start_blocks(*route(ents[d], lands[d], 2 + d))
         lands[d][me] = ents[d][me]
 
@@ -620,8 +601,8 @@
                 pltpu.VMEM((states * folds, LANES), f32),
                 pltpu.VMEM((rows * SUB, LANES), f32),
                 third, third, third, third, third, third,
-                pltpu.SemaphoreType.DMA((9, shards)),
-                pltpu.SemaphoreType.DMA((9, shards)),
+                pltpu.SemaphoreType.DMA((9,)),
+                pltpu.SemaphoreType.DMA((9,)),
                 pltpu.SemaphoreType.DMA((2,)),
                 pltpu.SemaphoreType.DMA((2,)),
                 pltpu.SemaphoreType.DMA((5,)),

time: 101 us -> 91.3 us (0.904)
  Pallas kernels: 96.8 us -> 87.4 us
    pallas_call x1, Pallas kernels: 96.8 us -> 87.4 us  [local(): pl.pallas_call(functools.partial(layer_kernel, shards, states, rank, chun...]
where the time goes in v5:
time: 91.3 us; the launch traced here: 91.1 us
  Pallas kernels  87.4 us (96%)
  local copies, waits for them, and re-layouts  2.31 us (3%)
  other arithmetic  1.31 us (1%)
    pallas_call x1, Pallas kernels, local(): pl.pallas_call(functools.partial(layer_kernel, shards, states, rank, chun...  87.4 us
    unnamed x1, local copies, waits for them, and re-layouts  2.06 us

profile of v5, /device:TPU:0, one launch (start us, length us, event | category | flops | bytes accessed | tf_op | source)
XLA Modules:
  0.0 91.1 jit_solution(4526224319032155163)
XLA Ops:
  0.0 0.7 fusion.1
  0.7 0.1 tile.10
  0.8 0.1 copy.13
  0.9 0.1 copy.14
  0.9 0.6 broadcast_select_fusion.slots_ref
  1.6 87.4 %layer.1 = bf16[128,3072]{1,0:T(8,128)(2,1)} custom-call(s32[4]{0:T(128)} %len_ref.1, bf16[128,1536]{1,0:T(8,128)(2,1)} %emb_ref.1, f32[32,1,128]{2,1,0:T(1,128)} %broadcast_select_fusion.slots_ref, f32[2,4,3072]{2,1,0:T(4,128)} %cw_ref.1, f32[2,3072]{1,0:T(2,128)} %cb_ref.1, f32[2,3072]{1,0:T(2,128)} %db_ref.1, f32[2,3072]{1,0:T(2,128)} %skip_ref.1, ...), custom_call_target="tpu_custom_call" | custom-call | tf_op jit(solution)/shard_map/layer/pallas_call | solution.py:565
  89.0 2.1 %copy.16 = bf16[128,3072]{1,0:T(8,128)(2,1)} copy(bf16[128,3072]{1,0:T(8,128)(2,1)} %layer.1) | data formatting | bytes 1572864
  (2 shorter events, 0.0 us)

commit v6 on v5

--- a/solution.py
+++ b/solution.py
@@ -135,7 +135,7 @@
                         y_ref[spot, :] += y
                     return (tuple(out), sdt + dt)
 
-                return lax.fori_loop(0, chunk, row_step, (hs, sdt), unroll=8)
+                return lax.fori_loop(0, chunk, row_step, (hs, sdt), unroll=16)
 
             hs, sdt = lax.fori_loop(0, chunks, chunk_step, ((zero,) * states, zero))
             keep_last(j, hs, sdt)
@@ -226,7 +226,7 @@
                 tot[spot, :] += y
             return sdt
 
-        return (alive, lax.fori_loop(0, chunk, row_step, sdt, unroll=8))
+        return (alive, lax.fori_loop(0, chunk, row_step, sdt, unroll=16))
 
     lax.fori_loop(
         0, chunks, chunk_step, (jnp.float32(1.0), jnp.zeros((SUB, LANES), jnp.float32))
@@ -278,7 +278,7 @@
         )
         return 0
 
-    lax.fori_loop(1, shards, greet, 0)
+    lax.fori_loop(1, shards, greet, 0, unroll=True)
 
 
 def await_all(shards):
@@ -294,7 +294,7 @@
         ).start()
         return 0
 
-    lax.fori_loop(1, shards, go, 0)
+    lax.fori_loop(1, shards, go, 0, unroll=True)
 
 
 def await_blocks(src, dst, me, shards, send_sem, recv_sem):

time: 91.3 us -> 89.9 us (0.985)
  Pallas kernels: 87.4 us -> 86.1 us
    pallas_call x1, Pallas kernels: 87.4 us -> 86.1 us  [local(): pl.pallas_call(functools.partial(layer_kernel, shards, states, rank, chun...]
where the time goes in v6:
time: 89.9 us; the launch traced here: 89.8 us
  Pallas kernels  86.1 us (96%)
  local copies, waits for them, and re-layouts  2.31 us (3%)
  other arithmetic  1.31 us (1%)
    pallas_call x1, Pallas kernels, local(): pl.pallas_call(functools.partial(layer_kernel, shards, states, rank, chun...  86.1 us
    unnamed x1, local copies, waits for them, and re-layouts  2.06 us

profile of v6, /device:TPU:0, one launch (start us, length us, event | category | flops | bytes accessed | tf_op | source)
XLA Modules:
  0.0 89.8 jit_solution(12879130081219483985)
XLA Ops:
  0.0 0.7 fusion.1
  0.7 0.1 tile.10
  0.8 0.1 copy.13
  0.9 0.1 copy.14
  0.9 0.6 broadcast_select_fusion.slots_ref
  1.6 86.1 %layer.1 = bf16[128,3072]{1,0:T(8,128)(2,1)} custom-call(s32[4]{0:T(128)} %len_ref.1, bf16[128,1536]{1,0:T(8,128)(2,1)} %emb_ref.1, f32[32,1,128]{2,1,0:T(1,128)} %broadcast_select_fusion.slots_ref, f32[2,4,3072]{2,1,0:T(4,128)} %cw_ref.1, f32[2,3072]{1,0:T(2,128)} %cb_ref.1, f32[2,3072]{1,0:T(2,128)} %db_ref.1, f32[2,3072]{1,0:T(2,128)} %skip_ref.1, ...), custom_call_target="tpu_custom_call" | custom-call | tf_op jit(solution)/shard_map/layer/pallas_call | solution.py:565
  87.7 2.1 %copy.16 = bf16[128,3072]{1,0:T(8,128)(2,1)} copy(bf16[128,3072]{1,0:T(8,128)(2,1)} %layer.1) | data formatting | bytes 1572864
  (2 shorter events, 0.0 us)
